TPU v7x, 32 devices: a whole 2x2x4 slice. The times are simulated.
32 devices in a mesh: dp: 4 (over y, core), ctx: 8 (over z, x).
Axes of the slice: x: 2, y: 2, z: 4, core: 2. Of those that a mesh axis runs over, the one named last changes fastest.
Arguments:
- tokens: bfloat16 [4, 1024, 1152], P('dp', 'ctx'), may hold values from -6 to 6
- positions: int32 [4, 1024], P('dp', 'ctx'), may hold values from 0 to 2046, as said below
- block_sizes: int32 [4], P('dp'), may hold values from 128 to 512, as said below
- attn_gain: bfloat16 [1152], P('ctx'), may hold values from 0.099609375 to 1.8984375
- w_query: bfloat16 [1152, 1152], P('ctx', 'dp'), may hold values from -0.25 to 0.25
- w_key: bfloat16 [1152, 384], P('ctx', 'dp'), may hold values from -0.25 to 0.25
- w_value: bfloat16 [1152, 384], P('ctx', 'dp'), may hold values from -0.1875 to 0.1875
- w_out: bfloat16 [1152, 1152], P('ctx', 'dp'), may hold values from -1.5 to 1.5
- mlp_gain: bfloat16 [1152], P('ctx'), may hold values from 0.099609375 to 1.8984375
- w_gate: bfloat16 [1152, 3072], P('ctx', 'dp'), may hold values from -0.1875 to 0.1875
- w_up: bfloat16 [1152, 3072], P('ctx', 'dp'), may hold values from -0.1875 to 0.1875
- w_down: bfloat16 [3072, 1152], P('ctx', 'dp'), may hold values from -0.109375 to 0.109375
- cotangent: bfloat16 [4, 1024, 1152], P('dp', 'ctx'), may hold values from -6 to 6
Outputs:
- output: bfloat16 [4, 1024, 1152], P('dp', 'ctx')
- input_grad: bfloat16 [4, 1024, 1152], P('dp', 'ctx')
- grad_attn_gain: float32 [1152], P('ctx')
- grad_w_query: float32 [1152, 1152], P('ctx', 'dp')
- grad_w_key: float32 [1152, 384], P('ctx', 'dp')
- grad_w_value: float32 [1152, 384], P('ctx', 'dp')
- grad_w_out: float32 [1152, 1152], P('ctx', 'dp')
- grad_mlp_gain: float32 [1152], P('ctx')
- grad_w_gate: float32 [1152, 3072], P('ctx', 'dp')
- grad_w_up: float32 [1152, 3072], P('ctx', 'dp')
- grad_w_down: float32 [3072, 1152], P('ctx', 'dp')
Inputs may be any that keep to these rules, and one draw needn't show every extreme that they name: `positions`: strictly increasing along each sequence in steps of 1 to 3, from 0 to 2046. `block_sizes`: every entry is 128, 256 or 512, and each of the three occurs.
All inputs are finite; a program needn't handle non-finite values.
Results may differ from a plain program's by a relative error of at most 0.02.
Values may be sent and summed in bfloat16 or wider, within the bound.
A program may use at most 256 MiB of HBM per device.

v0:
```python
import jax
import jax.numpy as jnp
from jax import lax
from jax.sharding import PartitionSpec as P

QUERY_HEADS = 18
KEY_VALUE_HEADS = 6
HEAD_SIZE = 64


EPSILON = 1e-05
THETA = 10000.0
VERY_NEGATIVE = -1e30


def product(left, right):
    return jnp.dot(left, right, preferred_element_type=jnp.float32)


def angles_of(place_ids):
    half_dim = HEAD_SIZE // 2
    frequency = THETA ** (-(jnp.arange(half_dim, dtype=jnp.float32) * 2.0 / HEAD_SIZE))
    return place_ids.astype(jnp.float32)[:, None] * frequency[None, :]


def rotate(values, angles, forward):
    row_total = values.shape[0]
    half_dim = angles.shape[1]
    shaped = values.reshape(row_total, -1, 2 * half_dim)
    first_half = shaped[..., :half_dim]
    second = shaped[..., half_dim:]
    cosine = jnp.cos(angles)[:, None, :]
    sine_vals = jnp.sin(angles)[:, None, :]
    if forward:
        rotated = jnp.concatenate(
            [first_half * cosine - second * sine_vals, second * cosine + first_half * sine_vals], -1
        )
    else:
        rotated = jnp.concatenate(
            [first_half * cosine + second * sine_vals, second * cosine - first_half * sine_vals], -1
        )
    return rotated.reshape(row_total, -1)


def norm_back(grad_normed, normed, inverse):
    return inverse * (grad_normed - normed * jnp.mean(grad_normed * normed, -1, keepdims=True))


def visible(query_rows, key_rows, block_len):
    return ((key_rows // block_len)[None, :] <= (query_rows // block_len)[:, None])[None, None]


def attend_forward(query_rows4, complete_keys, complete_values, query_rows, block_len, score_scale):
    key_count = complete_keys.shape[0]
    key_row_width = 512
    block_list = key_count // key_row_width
    query_group_width = QUERY_HEADS // KEY_VALUE_HEADS
    row_total = query_rows4.shape[0]
    key_block_list = complete_keys.reshape(block_list, key_row_width, KEY_VALUE_HEADS, HEAD_SIZE)
    value_block_list = complete_values.reshape(
        block_list, key_row_width, KEY_VALUE_HEADS, HEAD_SIZE
    )
    last_block = query_rows[-1] // block_len

    def advance(carried, inputs):
        key_blk, val_blk, first_key = inputs
        key_rows = first_key + jnp.arange(key_row_width, dtype=jnp.int32)

        def compute(current):
            run_max, run_sum, accum = current
            scores = (
                jnp.einsum(
                    "tkgd,nkd->kgtn", query_rows4, key_blk, preferred_element_type=jnp.float32
                )
                * score_scale
            )
            allowed = visible(query_rows, key_rows, block_len)
            scores = jnp.where(allowed, scores, VERY_NEGATIVE)
            new_max = jnp.maximum(run_max, jnp.max(scores, -1))
            weights = jnp.where(allowed, jnp.exp(scores - new_max[..., None]), 0.0)
            factor = jnp.exp(run_max - new_max)
            new_sum = run_sum * factor + jnp.sum(weights, -1)
            accum = accum * factor[..., None] + jnp.einsum(
                "kgtn,nkd->kgtd",
                weights.astype(jnp.bfloat16),
                val_blk,
                preferred_element_type=jnp.float32,
            )
            return (new_max, new_sum, accum)

        return (
            lax.cond(
                first_key // block_len > last_block, lambda unchanged: unchanged, compute, carried
            ),
            None,
        )

    start_state = (
        jnp.full((KEY_VALUE_HEADS, query_group_width, row_total), VERY_NEGATIVE, jnp.float32),
        jnp.zeros((KEY_VALUE_HEADS, query_group_width, row_total), jnp.float32),
        jnp.zeros((KEY_VALUE_HEADS, query_group_width, row_total, HEAD_SIZE), jnp.float32),
    )
    firsts = jnp.arange(block_list, dtype=jnp.int32) * key_row_width
    final_state, unused = lax.scan(advance, start_state, (key_block_list, value_block_list, firsts))
    run_max, run_sum, accum = final_state
    return (accum / run_sum[..., None], run_max + jnp.log(run_sum))


def attend_backward(
    query_rows4,
    head_gradients,
    log_sums,
    row_delta,
    complete_keys,
    complete_values,
    query_rows,
    block_len,
    score_scale,
):
    key_count = complete_keys.shape[0]
    key_row_width = 512
    block_list = key_count // key_row_width
    query_group_width = QUERY_HEADS // KEY_VALUE_HEADS
    row_total = query_rows4.shape[0]
    key_block_list = complete_keys.reshape(block_list, key_row_width, KEY_VALUE_HEADS, HEAD_SIZE)
    value_block_list = complete_values.reshape(
        block_list, key_row_width, KEY_VALUE_HEADS, HEAD_SIZE
    )
    last_block = query_rows[-1] // block_len

    def advance(grad_query, inputs):
        key_blk, val_blk, first_key = inputs
        key_rows = first_key + jnp.arange(key_row_width, dtype=jnp.int32)

        def compute(current):
            scores = (
                jnp.einsum(
                    "tkgd,nkd->kgtn", query_rows4, key_blk, preferred_element_type=jnp.float32
                )
                * score_scale
            )
            allowed = visible(query_rows, key_rows, block_len)
            prob_vals = jnp.where(allowed, jnp.exp(scores - log_sums[..., None]), 0.0)
            grad_prob = jnp.einsum(
                "tkgd,nkd->kgtn", head_gradients, val_blk, preferred_element_type=jnp.float32
            )
            grad_score = (prob_vals * (grad_prob - row_delta[..., None])).astype(jnp.bfloat16)
            current = current + jnp.einsum(
                "kgtn,nkd->tkgd", grad_score, key_blk, preferred_element_type=jnp.float32
            )
            grad_key = jnp.einsum(
                "kgtn,tkgd->nkd", grad_score, query_rows4, preferred_element_type=jnp.float32
            )
            grad_value = jnp.einsum(
                "kgtn,tkgd->nkd",
                prob_vals.astype(jnp.bfloat16),
                head_gradients,
                preferred_element_type=jnp.float32,
            )
            return (current, (grad_key, grad_value))

        def nothing(current):
            empty_block = jnp.zeros((key_row_width, KEY_VALUE_HEADS, HEAD_SIZE), jnp.float32)
            return (current, (empty_block, empty_block))

        return lax.cond(first_key // block_len > last_block, nothing, compute, grad_query)

    firsts = jnp.arange(block_list, dtype=jnp.int32) * key_row_width
    initial_gradient = jnp.zeros(
        (row_total, KEY_VALUE_HEADS, query_group_width, HEAD_SIZE), jnp.float32
    )
    grad_query, stacked_rows = lax.scan(
        advance, initial_gradient, (key_block_list, value_block_list, firsts)
    )
    key_gradients = stacked_rows[0].reshape(key_count, KEY_VALUE_HEADS * HEAD_SIZE)
    value_gradients = stacked_rows[1].reshape(key_count, KEY_VALUE_HEADS * HEAD_SIZE)
    return (grad_query, key_gradients, value_gradients)


def on_device(
    tokens,
    positions,
    block_sizes,
    attn_gain,
    w_query,
    w_key,
    w_value,
    w_out,
    mlp_gain,
    w_gate,
    w_up,
    w_down,
    cotangent,
):
    row_parts = (
        lax.all_gather(w_query, "ctx", axis=0, tiled=True),
        lax.all_gather(w_key, "ctx", axis=0, tiled=True),
        lax.all_gather(w_value, "ctx", axis=0, tiled=True),
        lax.all_gather(w_out, "ctx", axis=0, tiled=True),
        lax.all_gather(w_gate, "ctx", axis=0, tiled=True),
        lax.all_gather(w_up, "ctx", axis=0, tiled=True),
        lax.all_gather(w_down, "ctx", axis=0, tiled=True),
        lax.all_gather(attn_gain, "ctx", axis=0, tiled=True),
        lax.all_gather(mlp_gain, "ctx", axis=0, tiled=True),
    )
    whole_w = (
        lax.all_gather(row_parts[0], "dp", axis=1, tiled=True),
        lax.all_gather(row_parts[1], "dp", axis=1, tiled=True),
        lax.all_gather(row_parts[2], "dp", axis=1, tiled=True),
        lax.all_gather(row_parts[3], "dp", axis=1, tiled=True),
        lax.all_gather(row_parts[4], "dp", axis=1, tiled=True),
        lax.all_gather(row_parts[5], "dp", axis=1, tiled=True),
        lax.all_gather(row_parts[6], "dp", axis=1, tiled=True),
    )
    query_w, key_w, value_w, out_w, gate_w, up_w, down_w = whole_w
    gain_one = row_parts[7].astype(jnp.float32)
    gain_two = row_parts[8].astype(jnp.float32)
    seq_count = tokens.shape[0]
    seq_rows = tokens.shape[1]
    width = tokens.shape[2]
    inputs = tokens.reshape(seq_count * seq_rows, width).astype(jnp.float32)
    row_total = inputs.shape[0]
    query_group_width = QUERY_HEADS // KEY_VALUE_HEADS
    query_rows = lax.axis_index("ctx") * seq_rows + jnp.arange(seq_rows, dtype=jnp.int32)
    angles = angles_of(positions.reshape(-1))
    score_scale = HEAD_SIZE ** (-0.5)
    inv_one = lax.rsqrt(jnp.mean(inputs * inputs, -1, keepdims=True) + EPSILON)
    normed_one = inputs * inv_one
    hidden_one = (normed_one * gain_one).astype(jnp.bfloat16)
    query_matrix = rotate(product(hidden_one, query_w), angles, True).astype(jnp.bfloat16)
    keys_own = rotate(product(hidden_one, key_w), angles, True).astype(jnp.bfloat16)
    values_own = product(hidden_one, value_w).astype(jnp.bfloat16)
    complete_keys, complete_values = (
        lax.all_gather(keys_own.reshape(seq_count, seq_rows, -1), "ctx", axis=1, tiled=True),
        lax.all_gather(values_own.reshape(seq_count, seq_rows, -1), "ctx", axis=1, tiled=True),
    )
    query_rows4 = query_matrix.reshape(row_total, KEY_VALUE_HEADS, query_group_width, HEAD_SIZE)
    member = 0
    heads_one, lse_one = attend_forward(
        query_rows4,
        complete_keys[member],
        complete_values[member],
        query_rows,
        block_sizes[member],
        score_scale,
    )
    attn_flat = heads_one.transpose(2, 0, 1, 3).reshape(row_total, QUERY_HEADS * HEAD_SIZE)
    attn_low = attn_flat.astype(jnp.bfloat16)
    mixed_rows = inputs + product(attn_low, out_w)
    inv_two = lax.rsqrt(jnp.mean(mixed_rows * mixed_rows, -1, keepdims=True) + EPSILON)
    normed_two = mixed_rows * inv_two
    hidden_two = (normed_two * gain_two).astype(jnp.bfloat16)
    gate_pre = product(hidden_two, gate_w)
    up_pre = product(hidden_two, up_w)
    sigmoid_gate = jax.nn.sigmoid(gate_pre)
    silu_gate = gate_pre * sigmoid_gate
    inner_act = (silu_gate * up_pre).astype(jnp.bfloat16)
    result = mixed_rows + product(inner_act, down_w)
    output = result.astype(jnp.bfloat16).reshape(seq_count, seq_rows, width)
    back_parts = (
        lax.all_gather(w_query, "ctx", axis=0, tiled=True),
        lax.all_gather(w_key, "ctx", axis=0, tiled=True),
        lax.all_gather(w_value, "ctx", axis=0, tiled=True),
        lax.all_gather(w_out, "ctx", axis=0, tiled=True),
        lax.all_gather(w_gate, "ctx", axis=0, tiled=True),
        lax.all_gather(w_up, "ctx", axis=0, tiled=True),
        lax.all_gather(w_down, "ctx", axis=0, tiled=True),
    )
    back_whole = (
        lax.all_gather(back_parts[0], "dp", axis=1, tiled=True),
        lax.all_gather(back_parts[1], "dp", axis=1, tiled=True),
        lax.all_gather(back_parts[2], "dp", axis=1, tiled=True),
        lax.all_gather(back_parts[3], "dp", axis=1, tiled=True),
        lax.all_gather(back_parts[4], "dp", axis=1, tiled=True),
        lax.all_gather(back_parts[5], "dp", axis=1, tiled=True),
        lax.all_gather(back_parts[6], "dp", axis=1, tiled=True),
    )
    back_query, back_key, back_value, back_out, back_gate, back_up, back_down = back_whole
    grad_top = cotangent.reshape(row_total, width)
    grad_down = jnp.einsum("tf,td->fd", inner_act, grad_top, preferred_element_type=jnp.float32)
    grad_inner = jnp.einsum("td,fd->tf", grad_top, back_down, preferred_element_type=jnp.float32)
    grad_gate = (
        grad_inner * up_pre * sigmoid_gate * (1.0 + gate_pre * (1.0 - sigmoid_gate))
    ).astype(jnp.bfloat16)
    grad_upval = (grad_inner * silu_gate).astype(jnp.bfloat16)
    grad_gatew = jnp.einsum("td,tf->df", hidden_two, grad_gate, preferred_element_type=jnp.float32)
    grad_upw = jnp.einsum("td,tf->df", hidden_two, grad_upval, preferred_element_type=jnp.float32)
    grad_hidden_two = jnp.einsum(
        "tf,df->td", grad_gate, back_gate, preferred_element_type=jnp.float32
    ) + jnp.einsum("tf,df->td", grad_upval, back_up, preferred_element_type=jnp.float32)
    grad_gain_two = jnp.sum(grad_hidden_two * normed_two, 0)
    grad_mixed = grad_top.astype(jnp.float32) + norm_back(
        grad_hidden_two * gain_two, normed_two, inv_two
    )
    grad_branch = grad_mixed.astype(jnp.bfloat16)
    grad_outw = jnp.einsum("tq,td->qd", attn_low, grad_branch, preferred_element_type=jnp.float32)
    attention_gradient = jnp.einsum(
        "td,qd->tq", grad_branch, back_out, preferred_element_type=jnp.float32
    ).astype(jnp.bfloat16)
    head_gradients = attention_gradient.reshape(
        row_total, KEY_VALUE_HEADS, query_group_width, HEAD_SIZE
    )
    row_delta = jnp.einsum("tkgd,kgtd->kgt", head_gradients.astype(jnp.float32), heads_one)
    member = 0
    grad_q_one, grad_k_one, grad_v_one = attend_backward(
        query_rows4,
        head_gradients,
        lse_one,
        row_delta,
        complete_keys[member],
        complete_values[member],
        query_rows,
        block_sizes[member],
        score_scale,
    )
    key_grads = [grad_k_one]
    value_grads = [grad_v_one]
    grad_keys_all = jnp.stack(key_grads, 0)
    grad_values_all = jnp.stack(value_grads, 0)
    grad_keys_own, grad_values_own = (
        lax.psum_scatter(grad_keys_all, "ctx", scatter_dimension=1, tiled=True),
        lax.psum_scatter(grad_values_all, "ctx", scatter_dimension=1, tiled=True),
    )
    grad_keys_own = grad_keys_own.reshape(row_total, -1)
    grad_values_own = grad_values_own.reshape(row_total, -1)
    grad_query_raw = rotate(
        grad_q_one.reshape(row_total, QUERY_HEADS * HEAD_SIZE) * score_scale, angles, False
    ).astype(jnp.bfloat16)
    grad_key_raw = rotate(grad_keys_own * score_scale, angles, False).astype(jnp.bfloat16)
    grad_value_raw = grad_values_own.astype(jnp.bfloat16)
    grad_queryw = jnp.einsum(
        "td,tq->dq", hidden_one, grad_query_raw, preferred_element_type=jnp.float32
    )
    grad_keyw = jnp.einsum(
        "td,tq->dq", hidden_one, grad_key_raw, preferred_element_type=jnp.float32
    )
    grad_valuew = jnp.einsum(
        "td,tq->dq", hidden_one, grad_value_raw, preferred_element_type=jnp.float32
    )
    grad_hidden_one = jnp.einsum(
        "tq,dq->td", grad_query_raw, back_query, preferred_element_type=jnp.float32
    )
    grad_hidden_one = grad_hidden_one + jnp.einsum(
        "tq,dq->td", grad_key_raw, back_key, preferred_element_type=jnp.float32
    )
    grad_hidden_one = grad_hidden_one + jnp.einsum(
        "tq,dq->td", grad_value_raw, back_value, preferred_element_type=jnp.float32
    )
    grad_gain_one = jnp.sum(grad_hidden_one * normed_one, 0)
    grad_input = grad_mixed + norm_back(grad_hidden_one * gain_one, normed_one, inv_one)
    input_grad = grad_input.astype(jnp.bfloat16).reshape(seq_count, seq_rows, width)
    summed_rows = (
        lax.psum_scatter(grad_queryw, "ctx", scatter_dimension=0, tiled=True),
        lax.psum_scatter(grad_keyw, "ctx", scatter_dimension=0, tiled=True),
        lax.psum_scatter(grad_valuew, "ctx", scatter_dimension=0, tiled=True),
        lax.psum_scatter(grad_outw, "ctx", scatter_dimension=0, tiled=True),
        lax.psum_scatter(grad_gatew, "ctx", scatter_dimension=0, tiled=True),
        lax.psum_scatter(grad_upw, "ctx", scatter_dimension=0, tiled=True),
        lax.psum_scatter(grad_down, "ctx", scatter_dimension=0, tiled=True),
        lax.psum_scatter(grad_gain_one, "ctx", scatter_dimension=0, tiled=True),
        lax.psum_scatter(grad_gain_two, "ctx", scatter_dimension=0, tiled=True),
    )
    final_w = (
        lax.psum_scatter(
            summed_rows[0].astype(jnp.bfloat16), "dp", scatter_dimension=1, tiled=True
        ).astype(jnp.float32),
        lax.psum_scatter(
            summed_rows[1].astype(jnp.bfloat16), "dp", scatter_dimension=1, tiled=True
        ).astype(jnp.float32),
        lax.psum_scatter(
            summed_rows[2].astype(jnp.bfloat16), "dp", scatter_dimension=1, tiled=True
        ).astype(jnp.float32),
        lax.psum_scatter(
            summed_rows[3].astype(jnp.bfloat16), "dp", scatter_dimension=1, tiled=True
        ).astype(jnp.float32),
        lax.psum_scatter(
            summed_rows[4].astype(jnp.bfloat16), "dp", scatter_dimension=1, tiled=True
        ).astype(jnp.float32),
        lax.psum_scatter(
            summed_rows[5].astype(jnp.bfloat16), "dp", scatter_dimension=1, tiled=True
        ).astype(jnp.float32),
        lax.psum_scatter(
            summed_rows[6].astype(jnp.bfloat16), "dp", scatter_dimension=1, tiled=True
        ).astype(jnp.float32),
    )
    final_gains = lax.psum((summed_rows[7], summed_rows[8]), "dp")
    return (
        output,
        input_grad,
        final_gains[0],
        final_w[0],
        final_w[1],
        final_w[2],
        final_w[3],
        final_gains[1],
        final_w[4],
        final_w[5],
        final_w[6],
    )


def solution(mesh):
    placed = (
        P("dp", "ctx", None),
        P("dp", "ctx"),
        P("dp"),
        P("ctx"),
        P("ctx", "dp"),
        P("ctx", "dp"),
        P("ctx", "dp"),
        P("ctx", "dp"),
        P("ctx"),
        P("ctx", "dp"),
        P("ctx", "dp"),
        P("ctx", "dp"),
        P("dp", "ctx", None),
    )
    return jax.shard_map(
        on_device,
        mesh=mesh,
        in_specs=placed,
        out_specs=(
            P("dp", "ctx", None),
            P("dp", "ctx", None),
            P("ctx"),
            P("ctx", "dp"),
            P("ctx", "dp"),
            P("ctx", "dp"),
            P("ctx", "dp"),
            P("ctx"),
            P("ctx", "dp"),
            P("ctx", "dp"),
            P("ctx", "dp"),
        ),
        check_vma=False,
    )
```

profile of v0, /device:TPU:0, one launch (start us, length us, event | category | flops | bytes accessed | tf_op | source)
XLA Modules:
  0.0 1876.0 jit_solution(17597643595519216468)
XLA Ops:
  9.4 35.4 %all_gather.72 = bf16[1152,288]{1,0:T(8,128)(2,1)S(1)} all-gather(bf16[144,288]{1,0:T(8,128)(2,1)} %param.25), channel_id=1, replica_groups=mesh['dp'=4,'ctx'=8] {'ctx'}, dimensions={0}, use_global_device_ids=true | all-gather | bytes 746496 | tf_op jit(solution)/shard_map/all_gather | solution.py:196
  46.1 34.8 %all_gather.77 = bf16[1152,288]{1,0:T(8,128)(2,1)S(1)} all-gather(bf16[144,288]{1,0:T(8,128)(2,1)} %param.28), channel_id=1, replica_groups=mesh['dp'=4,'ctx'=8] {'ctx'}, dimensions={0}, use_global_device_ids=true | all-gather | bytes 746496 | tf_op jit(solution)/shard_map/all_gather | solution.py:199
  82.7 37.3 %all-gather.18.cloned.1.call-done = bf16[1152,768]{1,0:T(8,128)(2,1)} async-done(((bf16[144,768]{1,0:T(8,128)(2,1)}), bf16[1152,768]{1,0:T(8,128)(2,1)}) %all-gather.18.cloned.1.call-update) | async-done | bytes 1769488 | tf_op jit(solution)/shard_map/all_gather | solution.py:201
  120.1 48.3 %all-gather.22.cloned.1.call-done = bf16[3072,288]{0,1:T(8,128)(2,1)} async-done(((bf16[384,288]{0,1:T(8,128)(2,1)}), bf16[3072,288]{0,1:T(8,128)(2,1)}) %all-gather.22.cloned.1.call-update) | async-done | bytes 1769488 | tf_op jit(solution)/shard_map/all_gather | solution.py:202
  171.7 30.8 %all_gather.69 = bf16[1152,96]{1,0:T(8,128)(2,1)S(1)} all-gather(bf16[144,96]{1,0:T(8,128)(2,1)S(1)} %copy-done.32), channel_id=1, replica_groups=mesh['dp'=4,'ctx'=8] {'ctx'}, dimensions={0}, use_global_device_ids=true | all-gather | bytes 248832 | tf_op jit(solution)/shard_map/all_gather | solution.py:197
  204.5 18.8 %all-reduce.6 = (bf16[1152]{0:T(1024)(128)(2,1)S(1)}, bf16[1152]{0:T(1024)(128)(2,1)S(1)}) all-reduce(bf16[1152]{0:T(1024)(128)(2,1)S(1)} %dynamic-update-slice, bf16[1152]{0:T(1024)(128)(2,1)S(1)} %dynamic-update-slice.1), channel_id=1, replica_groups=mesh['dp'=4,'ctx'=8] {'ctx'}, use_global_device_ids=true, to_apply=%add | all-reduce | flops 2304 | bytes 9216
  233.5 28.8 %all_gather.71 = bf16[1,1024,384]{1,2,0:T(8,128)(2,1)S(1)} all-gather(bf16[1,128,384]{1,2,0:T(8,128)(2,1)S(1)} %bitcast.250), channel_id=1, replica_groups=mesh['dp'=4,'ctx'=8] {'ctx'}, dimensions={1}, use_global_device_ids=true | all-gather | bytes 884736 | tf_op jit(solution)/shard_map/all_gather | solution.py:234
  263.0 30.9 %all_gather.74 = bf16[1152,96]{1,0:T(8,128)(2,1)S(1)} all-gather(bf16[144,96]{1,0:T(8,128)(2,1)S(1)} %copy-done.33), channel_id=1, replica_groups=mesh['dp'=4,'ctx'=8] {'ctx'}, dimensions={0}, use_global_device_ids=true | all-gather | bytes 248832 | tf_op jit(solution)/shard_map/all_gather | solution.py:198
  294.1 14.0 all_gather.75
  309.4 32.1 %all-gather = bf16[1024,384]{1,0:T(8,128)(2,1)S(1)} all-gather(bf16[128,384]{1,0:T(8,128)(2,1)S(1)} %convolution_convert_fusion.1), channel_id=2, replica_groups=mesh['dp'=4,'ctx'=8] {'ctx'}, dimensions={0}, use_global_device_ids=true | all-gather | bytes 884736 | tf_op jit(solution)/shard_map/all_gather | solution.py:235
  346.8 15.8 while.37
  403.1 91.0 %while.38 = (s32[]{:T(128)}, f32[128,6,3,64]{0,3,2,1:T(8,128)S(1)}, f32[2,512,6,64]{1,0,3,2:T(2,128)}, f32[2,512,6,64]{1,0,3,2:T(2,128)}, s32[2]{0:T(128)}, /*in...) while((s32[]{:T(128)}, f32[128,6,3,64]{0,3,2,1:T(8,128)S(1)}, ...), condition=%wide.region_12.13_spmd.clone, body=%wide.region_9.12_spmd.clone.sunk | while | flops 766989952 | bytes 58037788 | solution.py:172
  408.0 14.2 conditional.7
  423.9 14.9 dynamic_update_slice.17
  440.8 14.9 dynamic_update_slice.18
  462.3 14.9 dynamic_update_slice.17
  479.2 14.9 dynamic_update_slice.18
  500.3 77.2 %reduce-scatter.27.cloned.1.call-done = f32[1,128,384]{1,2,0:T(8,128)} async-done(((f32[1,1024,384]{1,2,0:T(8,128)}), f32[1,128,384]{1,2,0:T(8,128)}) %reduce-scatter.27.cloned.1.call-update) | async-done | bytes 196624 | tf_op jit(solution)/shard_map/reduce_scatter | solution.py:321
  580.4 65.6 %reduce-scatter.29.cloned.1.call-done = f32[1,128,384]{1,2,0:T(8,128)} async-done(((f32[1,1024,384]{1,2,0:T(8,128)}), f32[1,128,384]{1,2,0:T(8,128)}) %reduce-scatter.29.cloned.1.call-update) | async-done | bytes 196624 | tf_op jit(solution)/shard_map/reduce_scatter | solution.py:322
  679.5 35.1 %reduce-scatter.33.cloned.1.call-done = f32[144,384]{1,0:T(8,128)} async-done(((f32[1152,384]{1,0:T(8,128)}), f32[144,384]{1,0:T(8,128)}) %reduce-scatter.33.cloned.1.call-update) | async-done | bytes 221200 | tf_op jit(solution)/shard_map/reduce_scatter | solution.py:354
  716.4 67.1 %reduce-scatter.35.cloned.1.call-done = f32[144,384]{1,0:T(8,128)} async-done(((f32[1152,384]{1,0:T(8,128)}), f32[144,384]{1,0:T(8,128)}) %reduce-scatter.35.cloned.1.call-update) | async-done | bytes 221200 | tf_op jit(solution)/shard_map/reduce_scatter | solution.py:355
  785.4 104.8 %reduce-scatter.31.cloned.1.call-done = f32[144,1152]{1,0:T(8,128)} async-done(((f32[1152,1152]{1,0:T(8,128)}), f32[144,1152]{1,0:T(8,128)}) %reduce-scatter.31.cloned.1.call-update) | async-done | bytes 663568 | tf_op jit(solution)/shard_map/reduce_scatter | solution.py:353
  892.5 105.5 %reduce-scatter.37.cloned.1.call-done = f32[144,1152]{1,0:T(8,128)} async-done(((f32[1152,1152]{1,0:T(8,128)}), f32[144,1152]{1,0:T(8,128)}) %reduce-scatter.37.cloned.1.call-update) | async-done | bytes 663568 | tf_op jit(solution)/shard_map/reduce_scatter | solution.py:356
  1000.2 230.1 %reduce-scatter.47.cloned.1.call-done = f32[384,1152]{1,0:T(8,128)} async-done(((f32[3072,1152]{1,0:T(8,128)}), f32[384,1152]{1,0:T(8,128)}) %reduce-scatter.47.cloned.1.call-update) | async-done | bytes 1769488 | tf_op jit(solution)/shard_map/reduce_scatter | solution.py:359
  1233.4 228.8 %reduce-scatter.39.cloned.1.call-done = f32[144,3072]{1,0:T(8,128)} async-done(((f32[1152,3072]{1,0:T(8,128)}), f32[144,3072]{1,0:T(8,128)}) %reduce-scatter.39.cloned.1.call-update) | async-done | bytes 1769488 | tf_op jit(solution)/shard_map/reduce_scatter | solution.py:357
  1467.7 226.3 %reduce-scatter.43.cloned.1.call-done = f32[144,3072]{1,0:T(8,128)} async-done(((f32[1152,3072]{1,0:T(8,128)}), f32[144,3072]{1,0:T(8,128)}) %reduce-scatter.43.cloned.1.call-update) | async-done | bytes 1769488 | tf_op jit(solution)/shard_map/reduce_scatter | solution.py:358
  1704.0 35.2 %all-reduce.4 = (f32[1152]{0:T(1024)S(1)}, f32[1152]{0:T(1024)S(1)}) all-reduce(f32[1152]{0:T(1024)S(1)} %get-tuple-element.783, f32[1152]{0:T(1024)S(1)} %copy-done.34), channel_id=5, replica_groups=mesh['dp'=4,'ctx'=8] {'ctx'}, use_global_device_ids=true, to_apply=%region_17.18.clone | all-reduce | flops 2304 | bytes 18432
  1749.6 13.3 reduce-scatter.49.cloned.1.call-done
  1764.7 22.9 %reduce-scatter.55.cloned.1.call-done = bf16[288,144]{1,0:T(8,128)(2,1)} async-done(((bf16[1152,144]{1,0:T(8,128)(2,1)}), bf16[288,144]{1,0:T(8,128)(2,1)}) %reduce-scatter.55.cloned.1.call-update) | async-done | bytes 82960
  1789.3 24.7 %reduce-scatter.57.cloned.1.call-done = bf16[288,384]{1,0:T(8,128)(2,1)} async-done(((bf16[1152,384]{1,0:T(8,128)(2,1)}), bf16[288,384]{1,0:T(8,128)(2,1)}) %reduce-scatter.57.cloned.1.call-update) | async-done | bytes 221200
  1816.1 24.6 %reduce-scatter.41.cloned.1.call-done = bf16[144,768]{1,0:T(8,128)(2,1)} async-done(((bf16[144,3072]{1,0:T(8,128)(2,1)}), bf16[144,768]{1,0:T(8,128)(2,1)}) %reduce-scatter.41.cloned.1.call-update) | async-done | bytes 221200 | tf_op jit(solution)/shard_map/reduce_scatter | solution.py:376
  1842.4 24.6 %reduce-scatter.45.cloned.1.call-done = bf16[144,768]{1,0:T(8,128)(2,1)} async-done(((bf16[144,3072]{1,0:T(8,128)(2,1)}), bf16[144,768]{1,0:T(8,128)(2,1)}) %reduce-scatter.45.cloned.1.call-update) | async-done | bytes 221200 | tf_op jit(solution)/shard_map/reduce_scatter | solution.py:379
  (277 shorter events, 191.3 us)
Async XLA Ops:
  7.2 75.0 %all-gather.14.cloned.1.call-start = ((), (), s32[]{:S(2)}) async-start(), calls=%async_computation.18 | async-start | bytes 1990656 | tf_op jit(solution)/shard_map/all_gather | solution.py:200
  7.9 112.1 %all-gather.18.cloned.1.call-start = ((), (), s32[]{:S(2)}) async-start(), calls=%async_computation.20 | async-start | bytes 1990656 | tf_op jit(solution)/shard_map/all_gather | solution.py:201
  8.7 159.7 %all-gather.22.cloned.1.call-start = ((), (), s32[]{:S(2)}) async-start(), calls=%async_computation.22 | async-start | bytes 1990656 | tf_op jit(solution)/shard_map/all_gather | solution.py:202
  9.4 334.5 %all-gather.10.cloned.1.call-start = ((), (), s32[]{:S(2)}) async-start(), calls=%async_computation.16 | async-start | bytes 3317760 | tf_op jit(solution)/shard_map/all_gather | solution.py:207
  46.0 125.8 %copy-start.32 = (bf16[144,96]{1,0:T(8,128)(2,1)S(1)}, bf16[144,96]{1,0:T(8,128)(2,1)}, u32[]{:S(2)}) copy-start(bf16[144,96]{1,0:T(8,128)(2,1)} %param.26) | copy-start | bytes 82948
  46.0 156.7 %copy-start.35 = (u32[32]{0:T(128)S(1)}, u32[32]{0:T(128)}, u32[]{:S(2)}) copy-start(u32[32]{0:T(128)} %constant.164) | copy-start | bytes 388
  46.0 158.0 %copy-start.36 = (bf16[144]{0:T(256)(128)(2,1)S(1)}, bf16[144]{0:T(256)(128)(2,1)}, u32[]{:S(2)}) copy-start(bf16[144]{0:T(256)(128)(2,1)} %param.24) | copy-start | bytes 868
  46.0 158.2 %copy-start.37 = (bf16[144]{0:T(256)(128)(2,1)S(1)}, bf16[144]{0:T(256)(128)(2,1)}, u32[]{:S(2)}) copy-start(bf16[144]{0:T(256)(128)(2,1)} %param.29) | copy-start | bytes 868
  46.0 177.3 %copy-start.2 = (bf16[1,128,1152]{2,1,0:T(8,128)(2,1)S(1)}, bf16[1,128,1152]{2,1,0:T(8,128)(2,1)}, u32[]{:S(2)}) copy-start(bf16[1,128,1152]{2,1,0:T(8,128)(2,1)} %param.21) | copy-start | bytes 884740
  46.0 177.5 %copy-start.38 = (s32[1,128]{1,0:T(1,128)S(1)}, s32[1,128]{1,0:T(1,128)}, u32[]{:S(2)}) copy-start(s32[1,128]{1,0:T(1,128)} %param.22) | copy-start | bytes 1540
  46.1 316.7 %all-gather.12.cloned.1.call-start = ((), (), s32[]{:S(2)}) async-start(), calls=%async_computation.17 | async-start | bytes 3317760 | tf_op jit(solution)/shard_map/all_gather | solution.py:210
  82.1 284.5 %all-gather.16.cloned.1.call-start = ((), (), s32[]{:S(2)}) async-start(), calls=%async_computation.19 | async-start | bytes 8847360 | tf_op jit(solution)/shard_map/all_gather | solution.py:211
  82.6 289.4 %all-gather.20.cloned.1.call-start = ((), (), s32[]{:S(2)}) async-start(), calls=%async_computation.21 | async-start | bytes 8847360 | tf_op jit(solution)/shard_map/all_gather | solution.py:212
  120.0 262.9 %all-gather.24.cloned.1.call-start = ((), (), s32[]{:S(2)}) async-start(), calls=%async_computation.23 | async-start | bytes 8847360 | tf_op jit(solution)/shard_map/all_gather | solution.py:213
  168.4 409.1 %reduce-scatter.27.cloned.1.call-start = ((), (), s32[]{:S(2)}) async-start(), calls=%async_computation.24 | async-start | bytes 1769472 | tf_op jit(solution)/shard_map/reduce_scatter | solution.py:321
  223.7 122.9 %copy-start.28 = (f32[128,32]{0,1:T(8,128)}, f32[128,32]{0,1:T(8,128)S(1)}, u32[]{:S(2)}) copy-start(f32[128,32]{0,1:T(8,128)S(1)} %get-tuple-element.860) | copy-start | bytes 49156
  497.7 148.3 %reduce-scatter.29.cloned.1.call-start = ((), (), s32[]{:S(2)}) async-start(), calls=%async_computation.25 | async-start | bytes 1769472 | tf_op jit(solution)/shard_map/reduce_scatter | solution.py:322
  500.3 214.3 %reduce-scatter.33.cloned.1.call-start = ((), (), s32[]{:S(2)}) async-start(), calls=%async_computation.27 | async-start | bytes 1990656 | tf_op jit(solution)/shard_map/reduce_scatter | solution.py:354
  580.3 203.2 %reduce-scatter.35.cloned.1.call-start = ((), (), s32[]{:S(2)}) async-start(), calls=%async_computation.28 | async-start | bytes 1990656 | tf_op jit(solution)/shard_map/reduce_scatter | solution.py:355
  648.6 241.6 %reduce-scatter.31.cloned.1.call-start = ((), (), s32[]{:S(2)}) async-start(), calls=%async_computation.26 | async-start | bytes 5971968 | tf_op jit(solution)/shard_map/reduce_scatter | solution.py:353
  652.2 345.7 %reduce-scatter.37.cloned.1.call-start = ((), (), s32[]{:S(2)}) async-start(), calls=%async_computation.29 | async-start | bytes 5971968 | tf_op jit(solution)/shard_map/reduce_scatter | solution.py:356
  655.8 574.6 %reduce-scatter.47.cloned.1.call-start = ((), (), s32[]{:S(2)}) async-start(), calls=%async_computation.34 | async-start | bytes 15925248 | tf_op jit(solution)/shard_map/reduce_scatter | solution.py:359
  663.0 799.2 %reduce-scatter.39.cloned.1.call-start = ((), (), s32[]{:S(2)}) async-start(), calls=%async_computation.30 | async-start | bytes 15925248 | tf_op jit(solution)/shard_map/reduce_scatter | solution.py:357
  671.2 1022.8 %reduce-scatter.43.cloned.1.call-start = ((), (), s32[]{:S(2)}) async-start(), calls=%async_computation.32 | async-start | bytes 15925248 | tf_op jit(solution)/shard_map/reduce_scatter | solution.py:358
  679.5 1067.0 %reduce-scatter.51.cloned.1.call-start = ((), (), s32[]{:S(2)}) async-start(), calls=%async_computation.36 | async-start | bytes 245760
  716.4 1031.7 %reduce-scatter.53.cloned.1.call-start = ((), (), s32[]{:S(2)}) async-start(), calls=%async_computation.37 | async-start | bytes 245760
  785.3 977.6 %reduce-scatter.49.cloned.1.call-start = ((), (), s32[]{:S(2)}) async-start(), calls=%async_computation.35 | async-start | bytes 737280
  892.4 895.2 %reduce-scatter.55.cloned.1.call-start = ((), (), s32[]{:S(2)}) async-start(), calls=%async_computation.38 | async-start | bytes 737280
  1000.2 813.8 %reduce-scatter.57.cloned.1.call-start = ((), (), s32[]{:S(2)}) async-start(), calls=%async_computation.39 | async-start | bytes 1105920
  1233.3 463.2 %copy-start.5 = (f32[128,1152]{1,0:T(8,128)S(1)}, f32[128,1152]{1,0:T(8,128)}, u32[]{:S(2)}) copy-start(f32[128,1152]{1,0:T(8,128)} %copy-done.4) | copy-start | bytes 1769476
  1233.3 607.3 %reduce-scatter.41.cloned.1.call-start = ((), (), s32[]{:S(2)}) async-start(), calls=%async_computation.31 | async-start | bytes 1105920 | tf_op jit(solution)/shard_map/reduce_scatter | solution.py:376
  1464.7 402.2 %reduce-scatter.45.cloned.1.call-start = ((), (), s32[]{:S(2)}) async-start(), calls=%async_computation.33 | async-start | bytes 1105920 | tf_op jit(solution)/shard_map/reduce_scatter | solution.py:379
  (32 other events, 563.4 us)
Sparse Core Ops, SparseCore 0:
  10.2 61.5 all-gather.13
  74.0 45.9 all-gather.17
  122.1 46.2 all-gather.21
  169.8 23.9 all-gather.9
  195.2 25.7 all-gather.11
  222.4 50.8 all-gather.15
  274.9 55.5 all-gather.19
  332.1 50.8 all-gather.23
  497.8 79.7 reduce-scatter.26
  581.2 64.6 reduce-scatter.28
  649.4 65.1 reduce-scatter.32
  718.3 65.1 reduce-scatter.34
  787.1 103.0 reduce-scatter.30
  894.1 103.7 reduce-scatter.36
  1001.4 228.9 reduce-scatter.46
  1233.9 228.2 reduce-scatter.38
  1465.7 228.2 reduce-scatter.42
  1696.9 18.8 reduce-scatter.50
  1718.7 19.7 reduce-scatter.52
  1740.8 22.0 reduce-scatter.48
  1765.5 22.0 reduce-scatter.54
  1790.1 23.8 reduce-scatter.56
  1816.8 23.8 reduce-scatter.40
  1843.1 23.8 reduce-scatter.44
where the time goes:
time: 1890 us; the launch traced here: 1880 us
  waiting for transfers between devices  1340 us (71%)
  blocking collectives  276 us (15%)
  local copies, waits for them, and re-layouts  102 us (5%)
  matrix products  88.2 us (5%)
  other arithmetic  28.6 us (2%)
  between operations  19.4 us (1%)
    reduce_scatter x1, waiting for transfers between devices, on_device(): lax.psum_scatter(grad_down, 'ctx', scatter_dimension=0, tiled=True)  230 us
    reduce_scatter x1, waiting for transfers between devices, on_device(): lax.psum_scatter(grad_gatew, 'ctx', scatter_dimension=0, tiled=True)  229 us
    reduce_scatter x1, waiting for transfers between devices, on_device(): lax.psum_scatter(grad_upw, 'ctx', scatter_dimension=0, tiled=True)  226 us
    reduce_scatter x1, waiting for transfers between devices, on_device(): lax.psum_scatter(grad_outw, 'ctx', scatter_dimension=0, tiled=True)  105 us
    reduce_scatter x1, waiting for transfers between devices, on_device(): lax.psum_scatter(grad_queryw, 'ctx', scatter_dimension=0, tiled=True)  105 us
    reduce_scatter x1, waiting for transfers between devices, on_device(): lax.psum_scatter(grad_keys_all, 'ctx', scatter_dimension=1, tiled=True)  77.2 us
    reduce_scatter x1, waiting for transfers between devices, on_device(): lax.psum_scatter(grad_valuew, 'ctx', scatter_dimension=0, tiled=True)  67.1 us
    reduce_scatter x1, waiting for transfers between devices, on_device(): lax.psum_scatter(grad_values_all, 'ctx', scatter_dimension=1, tiled=True)  65.6 us
  transfers between devices with their start and end apart: 24, of which 17 were waited for; matrix products, arithmetic and copies ran while one was open for 6% of the time, Pallas kernels for 0%

commit v1 on v0

--- a/solution.py
+++ b/solution.py
@@ -1,6 +1,8 @@
 import jax
 import jax.numpy as jnp
 from jax import lax
+from jax.experimental import pallas as pl
+from jax.experimental.pallas import tpu as pltpu
 from jax.sharding import PartitionSpec as P
 
 QUERY_HEADS = 18
@@ -399,6 +401,808 @@
     )
 
 
+MESH = pl.DeviceIdType.MESH
+F32 = jnp.float32
+BF16 = jnp.bfloat16
+
+
+def dot_nn(a, b):
+    return lax.dot_general(a, b, (((1,), (0,)), ((), ())), preferred_element_type=F32)
+
+
+def dot_nt(a, b):
+    return lax.dot_general(a, b, (((1,), (1,)), ((), ())), preferred_element_type=F32)
+
+
+def dot_tn(a, b):
+    return lax.dot_general(a, b, (((0,), (0,)), ((), ())), preferred_element_type=F32)
+
+
+class Wires:
+    def __init__(self, send_sems, recv_sems):
+        self.send_sems, self.recv_sems = send_sems, recv_sems
+        self.sends = 0
+        self.recvs = 0
+        self.pending = []
+
+    def slots(self, count):
+        first = self.recvs
+        self.recvs += count
+        return first
+
+    def send(self, src, dst, slot, device, is_self=None):
+        mine = self.sends
+        self.sends += 1
+        remote = pltpu.make_async_remote_copy(
+            src_ref=src,
+            dst_ref=dst,
+            send_sem=self.send_sems.at[mine],
+            recv_sem=self.recv_sems.at[slot],
+            device_id=device,
+            device_id_type=MESH,
+        )
+        if is_self is None:
+            remote.start()
+            finish = remote.wait_send
+        else:
+            local = pltpu.make_async_copy(src, dst, self.recv_sems.at[slot])
+
+            @pl.when(is_self)
+            def _():
+                local.start()
+
+            @pl.when(jnp.logical_not(is_self))
+            def _():
+                remote.start()
+
+            def finish():
+                @pl.when(jnp.logical_not(is_self))
+                def _():
+                    remote.wait_send()
+
+        self.pending.append(finish)
+        return finish
+
+    def keep(self, src, dst, slot):
+        pltpu.make_async_copy(src, dst, self.recv_sems.at[slot]).start()
+
+    def recv(self, dst, slot):
+        pltpu.make_async_copy(dst, dst, self.recv_sems.at[slot]).wait()
+
+    def done(self, finish):
+        finish()
+        self.pending.remove(finish)
+
+    def drain(self):
+        for finish in self.pending:
+            finish()
+        self.pending = []
+
+
+N_SEM = 224
+
+
+def layer_kernel(
+    tok, cot, cs, bias, wqkv, wo, wgu, wdt,
+    o_out, o_ing, o_gain, o_qkv, o_o, o_gu, o_dt,
+    csf, b2, x2, wqz, woz, wq, wok, wg8, wd8, c8, n8, n1, qf, kvf, kv, q6, p6, o6, ab,
+    mp, ml, mid, dmid, dmb, dm4, do6, act, pt, l1, s2, l2, l1o, s2o, l2o,
+    ggu, lgu, sgu, lf, gdt, lgd, sgd, ld, lo, lq, so, sq, lzo, lzq, dkv, lx, sx, lkz,
+    lg, sg, lgz, dqk, send_sems, recv_sems,
+):
+    net = Wires(send_sems, recv_sems)
+    dp = lax.axis_index("dp")
+    ctx = lax.axis_index("ctx")
+    y, c = dp // 2, lax.rem(dp, 2)
+    z, x = ctx // 2, lax.rem(ctx, 2)
+    z_hi, z_lo = z // 2, lax.rem(z, 2)
+    y_c = y + c - 2 * y * c
+    tokens, width = tok.shape
+    rows = wqkv.shape[0]
+    qcols = wo.shape[1]
+    kcols = (wqkv.shape[1] - qcols) // 2
+    ff = wdt.shape[1]
+    drows = wdt.shape[0]
+    qw = 2 * qcols
+    kw = 2 * kcols
+    groups = kw // HEAD_SIZE
+    per = QUERY_HEADS // KEY_VALUE_HEADS
+    heads = groups * per
+    keys = kv.shape[1]
+    n_ctx = keys // tokens
+    scale = HEAD_SIZE ** (-0.5)
+
+    def flip(a, h):
+        return 1 - a if h else a
+
+    def zat(k):
+        return (z, 2 * z_hi + 1 - z_lo, 2 * (1 - z_hi) + z_lo, 3 - z)[k]
+
+    def dev(yy, cc, zz, xx):
+        return (2 * yy + cc, 2 * zz + xx)
+
+    def off(value, step):
+        return pl.multiple_of(value * step, step)
+
+    partner = dev(y, 1 - c, z, x)
+
+    barrier = pltpu.get_barrier_semaphore()
+    for k in range(4):
+        for hx in range(2):
+            for hy in range(2):
+                for hc in range(2):
+                    if k + hx + hy + hc:
+                        pl.semaphore_signal(
+                            barrier, inc=1,
+                            device_id=dev(flip(y, hy), flip(c, hc), zat(k), flip(x, hx)),
+                            device_id_type=MESH,
+                        )
+    pl.semaphore_wait(barrier, 31)
+
+    r_tok = net.slots(3)
+    net.send(tok, x2, r_tok, partner)
+    net.send(cs, csf.at[pl.ds(tokens, tokens)], r_tok + 1, partner)
+    net.send(bias, b2.at[1], r_tok + 2, partner)
+    r_wqz, r_woz = net.slots(4), net.slots(4)
+    r_wq, r_wo = net.slots(16), net.slots(16)
+
+    def spread_qkv(k, src):
+        zs = zat(k)
+        for hx in range(2):
+            for hy in range(2):
+                net.send(
+                    src,
+                    wq.at[c, pl.ds(off(2 * zs + x, rows), rows)],
+                    r_wq + k * 4 + hx * 2 + c,
+                    dev(flip(y, hy), y, z, flip(x, hx)),
+                    is_self=(c == y) if hx + hy == 0 else None,
+                )
+
+    def spread_wo(k, src):
+        zs = zat(k)
+        core = zs // 2
+        for hx in range(2):
+            for hy in range(2):
+                net.send(
+                    src,
+                    wok.at[dp, pl.ds(off(2 * lax.rem(zs, 2) + x, rows), rows)],
+                    r_wo + lax.rem(zs, 2) * 8 + hx * 4 + hy * 2 + c,
+                    dev(flip(y, hy), core, z, flip(x, hx)),
+                    is_self=(c == core) if hx + hy == 0 else None,
+                )
+
+    for k in range(1, 4):
+        net.send(wqkv, wqz.at[k - 1], r_wqz + k, dev(y, c, zat(k), x))
+    spread_qkv(0, wqkv)
+    for k in range(1, 4):
+        net.send(wo, woz.at[k - 1], r_woz + k, dev(y, c, zat(k), x))
+
+    csf[0:tokens] = cs[...]
+    b2[0] = bias[...]
+
+    def normed(values):
+        v = values.astype(F32)
+        inv = lax.rsqrt(jnp.mean(v * v, -1, keepdims=True) + EPSILON)
+        return v * inv, inv
+
+    n1[0:tokens] = normed(tok[...])[0].astype(BF16)
+    net.recv(x2, r_tok)
+    n1[tokens : 2 * tokens] = normed(x2[...])[0].astype(BF16)
+    net.recv(csf.at[pl.ds(tokens, tokens)], r_tok + 1)
+    net.recv(b2.at[1], r_tok + 2)
+
+    for k in range(1, 4):
+        net.recv(wqz.at[k - 1], r_wqz + k)
+        spread_qkv(k, wqz.at[k - 1])
+
+    r_gu, r_wd = net.slots(8), net.slots(4)
+    for k in range(4):
+        for hx in range(2):
+            net.send(
+                wgu.at[:, :, pl.ds(off(flip(x, hx), ff), ff)],
+                wg8.at[:, pl.ds(off(ctx, rows), rows)],
+                r_gu + k * 2 + hx,
+                dev(y_c, c, zat(k), flip(x, hx)),
+                is_self=(c == 0) if k + hx == 0 else None,
+            )
+    wd_c = z_lo
+    wd_y = z_hi + wd_c - 2 * z_hi * wd_c
+    wd_home = jnp.logical_and(wd_c == c, wd_y == y)
+    for k in range(4):
+        net.send(
+            wdt,
+            wd8.at[pl.ds(off(dp, drows), drows)],
+            r_wd + dp,
+            dev(wd_y, wd_c, zat(k), x),
+            is_self=wd_home if k == 0 else None,
+        )
+    spread_wo(0, wo)
+    for k in range(1, 4):
+        net.recv(woz.at[k - 1], r_woz + k)
+        spread_wo(k, woz.at[k - 1])
+
+    def gather_start(buf, slot):
+        for h in range(1, 4):
+            net.send(buf.at[0], buf.at[2 * h], slot + h, dev(flip(y, h % 2), c, z, flip(x, h // 2)))
+        net.send(buf.at[0], buf.at[1], slot + 4, partner)
+
+    def gather_pass(buf, slot, h):
+        net.recv(buf.at[2 * h], slot + h)
+        net.send(buf.at[2 * h], buf.at[2 * h + 1], slot + 4 + h, partner)
+
+    c8[0] = cot[...]
+    r_c8 = net.slots(8)
+    gather_start(c8, r_c8)
+
+    lane = lax.broadcasted_iota(jnp.int32, (2 * tokens, 128), 1)
+    low_half = lax.rem(lane, HEAD_SIZE) < HEAD_SIZE // 2
+
+    def turn(tile, forward):
+        other = jnp.where(low_half, pltpu.roll(tile, 96, 1), pltpu.roll(tile, 32, 1))
+        turned = other * csf[:, 128:256]
+        return tile * csf[:, 0:128] + (turned if forward else -turned)
+
+    for k in range(4):
+        for hx in range(2):
+            for cc in range(2):
+                net.recv(
+                    wq.at[cc, pl.ds(off(2 * zat(k) + flip(x, hx), rows), rows)],
+                    r_wq + k * 4 + hx * 2 + cc,
+                )
+    qf[:, qw:] = jnp.zeros((2 * tokens, qf.shape[1] - qw), F32)
+    for part in range(2):
+        got = dot_nn(n1[...], wq[part])
+        qf[:, qcols * part : qcols * (part + 1)] = got[:, :qcols]
+        kvf[:, kcols * part : kcols * (part + 1)] = got[:, qcols : qcols + kcols]
+        kvf[:, kw + kcols * part : kw + kcols * (part + 1)] = got[:, qcols + kcols :]
+    for t in range(qf.shape[1] // 128):
+        qf[:, 128 * t : 128 * (t + 1)] = turn(qf[:, 128 * t : 128 * (t + 1)], True) * scale
+
+    def turn_keys(forward):
+        for t in range(kw // 128 + 1):
+            tile = kvf[:, 128 * t : 128 * (t + 1)]
+            kvf[:, 128 * t : 128 * (t + 1)] = jnp.where(
+                128 * t + lane < kw, turn(tile, forward), tile
+            )
+
+    turn_keys(True)
+    own_keys = pl.ds(off(ctx, tokens), tokens)
+    for s in range(2):
+        kv[s, own_keys] = kvf[s * tokens : (s + 1) * tokens].astype(BF16)
+    r_kz, r_kx = net.slots(4), net.slots(4)
+    for k in range(1, 4):
+        net.send(kv.at[:, own_keys], kv.at[:, own_keys], r_kz + k, dev(y, c, zat(k), x))
+    net.send(kv.at[:, own_keys], kv.at[:, own_keys], r_kx, dev(y, c, z, 1 - x))
+    for s in range(2):
+        for h in range(heads):
+            q6[s * groups + h // per, (h % per) * tokens : (h % per + 1) * tokens] = qf[
+                s * tokens : (s + 1) * tokens, HEAD_SIZE * h : HEAD_SIZE * (h + 1)
+            ].astype(BF16)
+    for h in range(1, 4):
+        gather_pass(c8, r_c8, h)
+    for k in range(1, 4):
+        part = pl.ds(off(2 * zat(k) + x, tokens), tokens)
+        net.recv(kv.at[:, part], r_kz + k)
+        net.send(kv.at[:, part], kv.at[:, part], r_kx + k, dev(y, c, z, 1 - x))
+    for k in range(4):
+        net.recv(kv.at[:, pl.ds(off(2 * zat(k) + 1 - x, tokens), tokens)], r_kx + k)
+
+    def attend(s, carry):
+        mask = b2[s][0:1, :]
+        for g in range(groups):
+            kg = kv[s, :, HEAD_SIZE * g : HEAD_SIZE * (g + 1)]
+            vg = kv[s, :, kw + HEAD_SIZE * g : kw + HEAD_SIZE * (g + 1)]
+            scores = dot_nt(q6[s * groups + g], kg) + mask
+            weights = jnp.exp(scores - jnp.max(scores, -1, keepdims=True))
+            probs = (weights * (1.0 / jnp.sum(weights, -1, keepdims=True))).astype(BF16)
+            p6[s * groups + g] = probs
+            got = dot_nn(probs, vg).astype(BF16)
+            o6[s * groups + g] = got
+            for i in range(per):
+                h = g * per + i
+                ab[pl.ds(off(s, tokens), tokens), HEAD_SIZE * h : HEAD_SIZE * (h + 1)] = got[
+                    i * tokens : (i + 1) * tokens
+                ]
+        return carry
+
+    lax.fori_loop(0, 2, attend, 0)
+
+    for zz in range(2):
+        for hx in range(2):
+            for hy in range(2):
+                for cc in range(2):
+                    part = 2 * flip(y, hy) + cc
+                    net.recv(
+                        wok.at[part, pl.ds(off(2 * zz + flip(x, hx), rows), rows)],
+                        r_wo + zz * 8 + hx * 4 + hy * 2 + cc,
+                    )
+    for part in range(4):
+        got = dot_nn(ab[:, 0:qw], wok[part])
+        for s in range(2):
+            mp[s, :, qcols * part : qcols * (part + 1)] = got[s * tokens : (s + 1) * tokens]
+    r_ml = net.slots(1)
+    mp_sent = net.send(mp.at[1], ml, r_ml, partner)
+    net.recv(ml, r_ml)
+    mid[...] = tok[...].astype(F32) + mp[0] + ml[...]
+    n8[0] = normed(mid[...])[0].astype(BF16)
+    r_n8 = net.slots(8)
+    gather_start(n8, r_n8)
+
+    for h in range(1, 4):
+        net.recv(c8.at[2 * h + 1], r_c8 + 4 + h)
+    net.recv(c8.at[1], r_c8 + 4)
+    for k in range(4):
+        for hx in range(2):
+            net.recv(
+                wg8.at[:, pl.ds(off(2 * zat(k) + flip(x, hx), rows), rows)], r_gu + k * 2 + hx
+            )
+    for part in range(4):
+        net.recv(wd8.at[pl.ds(drows * part, drows)], r_wd + part)
+    for h in range(1, 4):
+        gather_pass(n8, r_n8, h)
+    net.recv(n8.at[1], r_n8 + 4)
+    for h in range(1, 4):
+        net.recv(n8.at[2 * h + 1], r_n8 + 4 + h)
+
+    all_tokens = 8 * tokens
+
+    def feed(i, carry):
+        pair = pl.ds(2 * i, 2)
+        here = n8[pair].reshape(2 * tokens, width)
+        grad_inner = dot_nn(c8[pair].reshape(2 * tokens, width), wd8[...])
+        gate = dot_nn(here, wg8[0])
+        up = dot_nn(here, wg8[1])
+        sig = 1.0 / (1.0 + jnp.exp(-gate))
+        silu = gate * sig
+        dgate = (grad_inner * up * sig * (1.0 + gate * (1.0 - sig))).astype(BF16)
+        dup = (grad_inner * silu).astype(BF16)
+        at = off(i, 2 * tokens)
+        act[pl.ds(at, 2 * tokens)] = (silu * up).astype(BF16)
+        act[pl.ds(at + all_tokens, 2 * tokens)] = dgate
+        act[pl.ds(at + 2 * all_tokens, 2 * tokens)] = dup
+        pt[pair] = (dot_nt(dgate, wg8[0]) + dot_nt(dup, wg8[1])).astype(BF16).reshape(2, tokens, width)
+        return carry
+
+    lax.fori_loop(0, 4, feed, 0)
+
+    def reduce_start(part, land, slot):
+        return [net.send(part.at[2 * h + 1], land.at[h], slot + h, partner) for h in range(4)]
+
+    def reduce_pass(part, land, out, land2, slot):
+        for h in range(1, 4):
+            net.recv(land.at[h], slot + h)
+            out[h - 1] = (part[2 * h].astype(F32) + land[h].astype(F32)).astype(BF16)
+            net.send(
+                out.at[h - 1], land2.at[h - 1], slot + 4 + h,
+                dev(flip(y, h % 2), c, z, flip(x, h // 2)),
+            )
+        net.recv(land.at[0], slot)
+        return part[0].astype(F32) + land[0].astype(F32)
+
+    def reduce_end(land2, slot):
+        total = 0.0
+        for h in range(1, 4):
+            net.recv(land2.at[h - 1], slot + 4 + h)
+            total = total + land2[h - 1].astype(F32)
+        return total
+
+    def flat(ref, i):
+        return ref[:, :, pl.ds(off(i, 128), 128)].reshape(all_tokens, 128)
+
+    def grad_gu(i, carry):
+        left = flat(n8, i)
+        at = pl.ds(off(i, 128), 128)
+        ggu[0, at] = dot_tn(left, act[pl.ds(all_tokens, all_tokens)]).astype(BF16)
+        ggu[1, at] = dot_tn(left, act[pl.ds(2 * all_tokens, all_tokens)]).astype(BF16)
+        return carry
+
+    def grad_d(i, carry):
+        gdt[pl.ds(off(i, 128), 128)] = dot_tn(flat(c8, i), act[pl.ds(0, all_tokens)]).astype(BF16)
+        return carry
+
+    def feed_out(i, carry):
+        got = dot_nt(act[pl.ds(off(i, 2 * tokens), 2 * tokens)], wd8[...])
+        pt[pl.ds(2 * i, 2)] = got.astype(BF16).reshape(2, tokens, width)
+        return carry
+
+    r_dn = net.slots(8)
+    pt_sent = reduce_start(pt, l1, r_dn)
+    lax.fori_loop(0, width // 128, grad_d, 0)
+    dmid[...] = reduce_pass(pt, l1, s2, l2, r_dn)
+
+    gd_z = 2 * y_c + c
+    r_gd = net.slots(4)
+
+    def to_home(k):
+        return pltpu.make_async_remote_copy(
+            src_ref=gdt, dst_ref=lgd.at[k - 1],
+            send_sem=send_sems.at[N_SEM - 4 + k], recv_sem=recv_sems.at[r_gd + k],
+            device_id=dev(y, c, zat(k), x), device_id_type=MESH,
+        )
+
+    for k in range(1, 4):
+        @pl.when(zat(k) == gd_z)
+        def _(k=k):
+            to_home(k).start()
+
+    lax.fori_loop(0, width // 128, grad_gu, 0)
+    r_gz = net.slots(4)
+    for k in range(1, 4):
+        net.send(
+            ggu.at[:, pl.ds(off(zat(k), 2 * rows), 2 * rows)], lgu.at[k - 1], r_gz + k,
+            dev(y, c, zat(k), x),
+        )
+    for finish in pt_sent:
+        net.done(finish)
+    lax.fori_loop(0, 4, feed_out, 0)
+    r_out = net.slots(8)
+    reduce_start(pt, l1o, r_out)
+
+    total = dmid[...] + reduce_end(l2, r_dn)
+    normed_two, inv_two = normed(mid[...])
+    sg[0] = jnp.zeros(sg.shape[1:], F32)
+    sg[0, 1:2] = jnp.sum(total * normed_two, 0, keepdims=True)
+    dmid[...] = cot[...].astype(F32) + inv_two * (
+        total - normed_two * jnp.mean(total * normed_two, -1, keepdims=True)
+    )
+    dmb[0] = dmid[...].astype(BF16)
+    r_dm = net.slots(1)
+    net.send(dmb.at[0], dmb.at[1], r_dm, partner)
+    mid[...] = mid[...] + reduce_pass(pt, l1o, s2o, l2o, r_out)
+    net.recv(dmb.at[1], r_dm)
+
+    for part in range(4):
+        for s in range(2):
+            dm4[part, s * tokens : (s + 1) * tokens] = dmb[s, :, qcols * part : qcols * (part + 1)]
+    dattn = dot_nt(dm4[0], wok[0])
+    for part in range(1, 4):
+        dattn = dattn + dot_nt(dm4[part], wok[part])
+    qf[:, 0:qw] = dattn
+    for s in range(2):
+        for h in range(heads):
+            do6[s * groups + h // per, (h % per) * tokens : (h % per + 1) * tokens] = qf[
+                s * tokens : (s + 1) * tokens, HEAD_SIZE * h : HEAD_SIZE * (h + 1)
+            ].astype(BF16)
+    attn_all = ab[:, 0:qw]
+    for part in range(4):
+        act[qw * part : qw * (part + 1), 0:qcols] = dot_tn(attn_all, dm4[part]).astype(BF16)
+    r_go = net.slots(16)
+    for zz in range(2):
+        for hx in range(2):
+            for hy in range(2):
+                for hc in range(2):
+                    zt = 2 * c + zz
+                    to_dp = 2 * flip(y, hy) + flip(c, hc)
+                    at = pl.multiple_of(to_dp * qw + (2 * zz + flip(x, hx)) * rows, rows)
+                    src = act.at[pl.ds(at, rows)]
+                    dst = lo.at[zt, hx * 2 + hy]
+                    slot = r_go + zt * 4 + hx * 2 + hy
+                    if hx + hy + hc == 0:
+                        net.keep(src, dst, slot)
+                    else:
+                        net.send(src, dst, slot, dev(flip(y, hy), flip(c, hc), z, flip(x, hx)))
+
+    def attend_back(s, carry):
+        for g in range(groups):
+            at = s * groups + g
+            kg = kv[s, :, HEAD_SIZE * g : HEAD_SIZE * (g + 1)]
+            vg = kv[s, :, kw + HEAD_SIZE * g : kw + HEAD_SIZE * (g + 1)]
+            dout = do6[at]
+            delta = jnp.sum(dout.astype(F32) * o6[at].astype(F32), -1, keepdims=True)
+            dprob = dot_nt(dout, vg)
+            dscore = (p6[at].astype(F32) * (dprob - delta)).astype(BF16)
+            dquery = dot_nn(dscore, kg) * scale
+            dkeys = dot_tn(q6[at], dscore)
+            dvals = dot_tn(dout, p6[at])
+            for t in range(n_ctx):
+                cols = slice(t * tokens, (t + 1) * tokens)
+                dkv[t, s, HEAD_SIZE * g : HEAD_SIZE * (g + 1)] = dkeys[:, cols].astype(BF16)
+                dkv[t, s, kw + HEAD_SIZE * g : kw + HEAD_SIZE * (g + 1)] = dvals[:, cols].astype(BF16)
+            for i in range(per):
+                h = g * per + i
+                qf[pl.ds(off(s, tokens), tokens), HEAD_SIZE * h : HEAD_SIZE * (h + 1)] = dquery[
+                    i * tokens : (i + 1) * tokens
+                ]
+        return carry
+
+    lax.fori_loop(0, 2, attend_back, 0)
+    r_dx, r_dz = net.slots(4), net.slots(4)
+    for k in range(4):
+        net.send(dkv.at[2 * zat(k) + 1 - x], lx.at[k], r_dx + k, dev(y, c, z, 1 - x))
+    for t in range(qf.shape[1] // 128):
+        qf[:, 128 * t : 128 * (t + 1)] = turn(qf[:, 128 * t : 128 * (t + 1)], False)
+    for part in range(2):
+        dqk[part, :, 0:qcols] = qf[:, qcols * part : qcols * (part + 1)].astype(BF16)
+    for k in range(1, 4):
+        net.recv(lx.at[k], r_dx + k)
+        sx[k - 1] = (dkv[2 * zat(k) + x].astype(F32) + lx[k].astype(F32)).astype(BF16)
+        net.send(sx.at[k - 1], lkz.at[k - 1], r_dz + k, dev(y, c, zat(k), x))
+
+    r_gf, r_ld = net.slots(2), net.slots(1)
+    mine = ggu[:, pl.ds(off(z, 2 * rows), 2 * rows)].astype(F32)
+    for k in range(1, 4):
+        net.recv(lgu.at[k - 1], r_gz + k)
+        mine = mine + lgu[k - 1].astype(F32)
+    sgu[...] = mine.astype(BF16)
+    for hx in range(2):
+        net.send(
+            sgu.at[:, pl.ds(off(flip(x, hx), rows), rows)], lf.at[hx], r_gf + hx,
+            dev(y_c, c, z, flip(x, hx)), is_self=(c == 0) if hx == 0 else None,
+        )
+
+    def share(hy, hc):
+        to_dp = 2 * flip(y, hy) + flip(c, hc)
+        return pltpu.make_async_remote_copy(
+            src_ref=sgd.at[pl.ds(off(to_dp, drows), drows)], dst_ref=ld,
+            send_sem=send_sems.at[N_SEM - 8 + 2 * hy + hc], recv_sem=recv_sems.at[r_ld],
+            device_id=dev(flip(y, hy), flip(c, hc), z, x), device_id_type=MESH,
+        )
+
+    @pl.when(z == gd_z)
+    def _():
+        for k in range(1, 4):
+            net.recv(lgd.at[k - 1], r_gd + k)
+
+        def add(i, carry):
+            at = pl.ds(off(i, 128), 128)
+            part = gdt[at].astype(F32)
+            for k in range(3):
+                part = part + lgd[k, at].astype(F32)
+            sgd[at] = part.astype(BF16)
+            return carry
+
+        lax.fori_loop(0, width // 128, add, 0)
+        net.keep(sgd.at[pl.ds(off(dp, drows), drows)], ld, r_ld)
+        for hy, hc in ((0, 1), (1, 0), (1, 1)):
+            share(hy, hc).start()
+
+    def attn_pass(land, out, send_at, slot, absolute):
+        for k in (1, 2, 3, 0):
+            at = zat(k) if absolute else k
+            part = 0.0
+            for h in range(4):
+                net.recv(land.at[at, h], slot + at * 4 + h)
+                part = part + land[at, h, :, 0 : out.shape[1]].astype(F32)
+            if k == 0:
+                out[...] = part
+            else:
+                send_at[0][k - 1] = part.astype(BF16)
+                net.send(send_at[0].at[k - 1], send_at[1].at[k - 1], send_at[2] + k, dev(y, c, zat(k), x))
+
+    r_zo, r_zq = net.slots(4), net.slots(4)
+    attn_pass(lo, o_o, (so, lzo, r_zo), r_go, True)
+
+    net.recv(lx.at[0], r_dx)
+    total = dkv[2 * z + x].astype(F32) + lx[0].astype(F32)
+    for k in range(1, 4):
+        net.recv(lkz.at[k - 1], r_dz + k)
+        total = total + lkz[k - 1].astype(F32)
+    for s in range(2):
+        kvf[s * tokens : (s + 1) * tokens] = total[s].T
+    turn_keys(False)
+    for part in range(2):
+        dqk[part, :, qcols : qcols + kcols] = kvf[:, kcols * part : kcols * (part + 1)].astype(BF16)
+        dqk[part, :, qcols + kcols :] = kvf[:, kw + kcols * part : kw + kcols * (part + 1)].astype(BF16)
+    for part in range(2):
+        got = dot_tn(n1[...], dqk[part]).astype(BF16)
+        for t in range(n_ctx):
+            p6[t // 2, (t % 2) * rows : (t % 2 + 1) * rows, 512 * part : 512 * part + qcols + 2 * kcols] = got[
+                rows * t : rows * (t + 1)
+            ]
+    r_gq = net.slots(16)
+    hy_c = y_c
+    for k in (1, 2, 3, 0):
+        for hx in range(2):
+            for ct in range(2):
+                net.send(
+                    p6.at[zat(k), pl.ds(off(flip(x, hx), rows), rows), pl.ds(512 * ct, 512)],
+                    lq.at[k, hx * 2 + hy_c],
+                    r_gq + k * 4 + hx * 2 + hy_c,
+                    dev(c, ct, z, flip(x, hx)),
+                    is_self=jnp.logical_and(y == c, c == ct) if hx == 0 else None,
+                )
+    net.done(mp_sent)
+    got = dot_nt(dqk[0], wq[0]) + dot_nt(dqk[1], wq[1])
+    for s in range(2):
+        mp[s] = got[s * tokens : (s + 1) * tokens]
+    r_dn1 = net.slots(1)
+    net.send(mp.at[1], ml, r_dn1, partner)
+    net.recv(ml, r_dn1)
+    total = mp[0] + ml[...]
+    normed_one, inv_one = normed(tok[...])
+    sg[0, 0:1] = jnp.sum(total * normed_one, 0, keepdims=True)
+    r_lg = net.slots(8)
+    for h in range(1, 8):
+        net.send(
+            sg.at[0], lg.at[h], r_lg + h, dev(flip(y, (h // 2) % 2), flip(c, h % 2), z, flip(x, h // 4))
+        )
+    o_ing[...] = (
+        dmid[...]
+        + inv_one * (total - normed_one * jnp.mean(total * normed_one, -1, keepdims=True))
+    ).astype(BF16)
+    gains = sg[0]
+    for h in range(1, 8):
+        net.recv(lg.at[h], r_lg + h)
+        gains = gains + lg[h]
+    sg[1] = gains
+    r_lgz = net.slots(4)
+    for k in range(1, 4):
+        net.send(sg.at[1], lgz.at[k - 1], r_lgz + k, dev(y, c, zat(k), x))
+
+    attn_pass(lq, o_qkv, (sq, lzq, r_zq), r_gq, False)
+
+    o_out[...] = (mid[...] + reduce_end(l2o, r_out)).astype(BF16)
+    for hx in range(2):
+        net.recv(lf.at[hx], r_gf + hx)
+        o_gu[:, :, pl.ds(off(flip(x, hx), ff), ff)] = lf[hx].astype(F32)
+    net.recv(ld, r_ld)
+    o_dt[...] = ld[...].astype(F32)
+    for out, land, slot in ((o_o, lzo, r_zo), (o_qkv, lzq, r_zq)):
+        for k in range(1, 4):
+            net.recv(land.at[k - 1], slot + k)
+            out[...] = out[...] + land[k - 1].astype(F32)
+    gains = sg[1]
+    for k in range(1, 4):
+        net.recv(lgz.at[k - 1], r_lgz + k)
+        gains = gains + lgz[k - 1]
+    o_gain[...] = gains
+
+    for k in range(1, 4):
+        @pl.when(zat(k) == gd_z)
+        def _(k=k):
+            to_home(k).wait_send()
+
+    @pl.when(z == gd_z)
+    def _():
+        for hy, hc in ((0, 1), (1, 0), (1, 1)):
+            share(hy, hc).wait_send()
+
+    net.drain()
+
+
+def run_layer(tok, cot, cs, bias, wqkv, wo, wgu, wdt):
+    tokens, width = tok.shape
+    rows, packed = wqkv.shape
+    qcols = wo.shape[1]
+    drows, ff = wdt.shape
+    keys = bias.shape[1]
+    n_ctx = keys // tokens
+    qw = 2 * qcols
+    kw = packed - qcols
+    groups = kw // HEAD_SIZE
+    per = QUERY_HEADS // KEY_VALUE_HEADS
+    stack = per * tokens
+    wide = -(-qw // 128) * 128
+    out_shape = [
+        jax.ShapeDtypeStruct((tokens, width), BF16),
+        jax.ShapeDtypeStruct((tokens, width), BF16),
+        jax.ShapeDtypeStruct((8, width), F32),
+        jax.ShapeDtypeStruct((rows, packed), F32),
+        jax.ShapeDtypeStruct((rows, qcols), F32),
+        jax.ShapeDtypeStruct((2, rows, 2 * ff), F32),
+        jax.ShapeDtypeStruct((drows, ff), F32),
+    ]
+
+    def vm(*shape, dtype=BF16):
+        return pltpu.VMEM(shape, dtype)
+
+    scratch = [
+        vm(2 * tokens, 256, dtype=F32),
+        vm(2, 8, keys, dtype=F32),
+        vm(tokens, width),
+        vm(3, rows, packed),
+        vm(3, rows, qcols),
+        vm(2, width, packed),
+        vm(4, 4 * rows, qcols),
+        vm(2, width, ff),
+        vm(width, ff),
+        vm(8, tokens, width),
+        vm(8, tokens, width),
+        vm(2 * tokens, width),
+        vm(2 * tokens, wide, dtype=F32),
+        vm(2 * tokens, 2 * kw, dtype=F32),
+        vm(2, keys, 2 * kw),
+        vm(2 * groups, stack, HEAD_SIZE),
+        vm(2 * groups, stack, keys),
+        vm(2 * groups, stack, HEAD_SIZE),
+        vm(2 * tokens, wide),
+        vm(2, tokens, width, dtype=F32),
+        vm(tokens, width, dtype=F32),
+        vm(tokens, width, dtype=F32),
+        vm(tokens, width, dtype=F32),
+        vm(2, tokens, width),
+        vm(4, 2 * tokens, qcols),
+        vm(2 * groups, stack, HEAD_SIZE),
+        vm(24 * tokens, ff),
+        vm(8, tokens, width),
+        vm(4, tokens, width),
+        vm(3, tokens, width),
+        vm(3, tokens, width),
+        vm(4, tokens, width),
+        vm(3, tokens, width),
+        vm(3, tokens, width),
+        vm(2, width, ff),
+        vm(3, 2, 2 * rows, ff),
+        vm(2, 2 * rows, ff),
+        vm(2, 2, rows, ff),
+        vm(width, ff),
+        vm(3, width, ff),
+        vm(width, ff),
+        vm(drows, ff),
+        vm(4, 4, rows, ff),
+        vm(4, 4, rows, 512),
+        vm(3, rows, qcols),
+        vm(3, rows, packed),
+        vm(3, rows, qcols),
+        vm(3, rows, packed),
+        vm(n_ctx, 2, 2 * kw, tokens),
+        vm(4, 2, 2 * kw, tokens),
+        vm(3, 2, 2 * kw, tokens),
+        vm(3, 2, 2 * kw, tokens),
+        vm(8, 8, width, dtype=F32),
+        vm(2, 8, width, dtype=F32),
+        vm(3, 8, width, dtype=F32),
+        vm(2, 2 * tokens, packed),
+        pltpu.SemaphoreType.DMA((N_SEM,)),
+        pltpu.SemaphoreType.DMA((N_SEM,)),
+    ]
+    inside = pl.BlockSpec(memory_space=pltpu.VMEM)
+    return pl.pallas_call(
+        layer_kernel,
+        out_shape=out_shape,
+        in_specs=[inside] * 8,
+        out_specs=[inside] * len(out_shape),
+        scratch_shapes=scratch,
+        compiler_params=pltpu.CompilerParams(
+            collective_id=0, has_side_effects=True, vmem_limit_bytes=VMEM_LIMIT
+        ),
+        name="layer",
+    )(tok, cot, cs, bias, wqkv, wo, wgu, wdt)
+
+
+VMEM_LIMIT = 63 * 1024 * 1024
+
+
+def on_device_plane(
+    tokens, positions, block_sizes, attn_gain, w_query, w_key, w_value, w_out, mlp_gain,
+    w_gate, w_up, w_down, cotangent,
+):
+    seq_rows, width = tokens.shape[1:]
+    ctx = lax.axis_index("ctx")
+    angles = angles_of(positions[0])
+    cosine, sine = jnp.cos(angles), jnp.sin(angles)
+    cs = jnp.concatenate([cosine] * 4 + [-sine, sine] * 2, 1)
+    keys = seq_rows * lax.axis_size("ctx")
+    block = block_sizes[0]
+    limit = (ctx * seq_rows // block + 1) * block
+    bias = jnp.where(jnp.arange(keys, dtype=jnp.int32) < limit, 0.0, VERY_NEGATIVE).astype(F32)
+    bias = jnp.broadcast_to(bias[None, :], (8, keys))
+    gain_one = attn_gain.astype(F32)[:, None]
+    gain_two = mlp_gain.astype(F32)[:, None]
+    wqkv = (jnp.concatenate([w_query, w_key, w_value], 1).astype(F32) * gain_one).astype(BF16)
+    wgu = jnp.stack([(w_gate.astype(F32) * gain_two).astype(BF16), (w_up.astype(F32) * gain_two).astype(BF16)])
+    output, input_grad, gains, g_qkv, g_o, g_gu, g_dt = run_layer(
+        tokens[0], cotangent[0], cs, bias, wqkv, w_out, wgu, w_down.T
+    )
+    rows, qcols = w_query.shape
+    kcols = w_key.shape[1]
+    part = lax.dynamic_slice(gains, (0, ctx * rows), (2, rows))
+    g_qkv = g_qkv * gain_one
+    return (
+        output[None],
+        input_grad[None],
+        part[0] / gain_one[:, 0],
+        g_qkv[:, :qcols],
+        g_qkv[:, qcols : qcols + kcols],
+        g_qkv[:, qcols + kcols :],
+        g_o,
+        part[1] / gain_two[:, 0],
+        g_gu[0] * gain_two,
+        g_gu[1] * gain_two,
+        g_dt.T,
+    )
+
+
 def solution(mesh):
     placed = (
         P("dp", "ctx", None),
@@ -415,8 +1219,9 @@
         P("ctx", "dp"),
         P("dp", "ctx", None),
     )
+    fits = mesh.shape["dp"] == 4 and mesh.shape["ctx"] == 8
     return jax.shard_map(
-        on_device,
+        on_device_plane if fits else on_device,
         mesh=mesh,
         in_specs=placed,
         out_specs=(

time: 1890 us -> 301 us (0.16)
  waiting for transfers between devices: 1340 us -> 0 us
  Pallas kernels: 0 us -> 285 us
  blocking collectives: 276 us -> 0 us
  local copies, waits for them, and re-layouts: 102 us -> 7.81 us
  matrix products: 88.2 us -> 0 us
  other arithmetic: 28.6 us -> 5.6 us
    reduce_scatter x11 -> x0, waiting for transfers between devices: 1190 us -> none  [the longest x1 230 us: on_device(): lax.psum_scatter(grad_down, 'ctx', scatter_dimension=0, tiled=True)]
    pallas_call x0 -> x1, Pallas kernels: none -> 285 us  [run_layer(): pl.pallas_call(layer_kernel, out_shape=out_shape, in_specs=[inside] * 8,...]
    all_gather x8 -> x0, blocking collectives: 216 us -> none  [the longest x1 35.4 us: on_device(): lax.all_gather(w_query, 'ctx', axis=0, tiled=True)]
    all_gather x8 -> x0, waiting for transfers between devices: 91.1 us -> none  [the longest x1 48.3 us: on_device(): lax.all_gather(w_down, 'ctx', axis=0, tiled=True)]
    dot_general x28 -> x0, matrix products: 88.2 us -> none  [the longest x7 24 us: product(): return jnp.dot(left, right, preferred_element_type=jnp.float32)]
    dynamic_update_slice x8 -> x0, local copies, waits for them, and re-layouts: 65.2 us -> none  [attend_backward(): lax.scan(advance, initial_gradient, (key_block_list, value_block_list, fi...]
    unnamed x29 -> x0, waiting for transfers between devices: 63.8 us -> none
    unnamed x2 -> x0, blocking collectives: 54 us -> none
  transfers between devices with their start and end apart: 24 -> 0, of which waited for: 17 -> 0; matrix products, arithmetic and copies ran while one was open for 6% -> 0% of each run, Pallas kernels for 0% -> 0%
where the time goes in v1:
time: 301 us; the launch traced here: 300 us
  Pallas kernels  285 us (95%)
  local copies, waits for them, and re-layouts  7.81 us (3%)
  other arithmetic  5.6 us (2%)
    pallas_call x1, Pallas kernels, run_layer(): pl.pallas_call(layer_kernel, out_shape=out_shape, in_specs=[inside] * 8,...  285 us

profile of v1, /device:TPU:0, one launch (start us, length us, event | category | flops | bytes accessed | tf_op | source)
XLA Modules:
  0.0 300.1 jit_solution(11270156173313805362)
XLA Ops:
  1.3 0.0 copy-start.11
  1.3 0.0 copy-start.9
  1.3 0.0 copy-start.10
  1.3 0.0 copy-start.7
  1.3 0.0 copy-start.8
  1.4 0.6 copy-done.11
  2.0 0.0 copy-done.9
  2.0 0.0 copy-done.10
  2.0 0.6 broadcast_in_dim.26.bias
  2.6 0.0 copy-done.7
  2.6 1.7 multiply_convert_fusion.2.wqkv
  4.3 0.3 multiply_sine_fusion
  4.6 0.0 copy-start.4
  4.6 0.0 copy-start.5
  4.7 0.8 concatenate.6.cs
  5.5 0.1 copy-done.4
  5.6 0.1 copy-done.5
  5.7 0.1 fusion
  5.8 0.8 pad_maximum_fusion.wgu
  6.6 285.2 %layer.1 = (bf16[128,1152]{1,0:T(8,128)(2,1)}, bf16[128,1152]{1,0:T(8,128)(2,1)}, f32[8,1152]{1,0:T(8,128)}, f32[144,480]{1,0:T(8,128)}, f32[144,288]{1,0:T(8,12...) custom-call(bf16[128,1152]{1,0:T(8,128)(2,1)} %bitcast.24, bf16[128,1152]{1,0:T(8,128)(2,1)} %bitcast.25, ...), custom_call_target="tpu_custom_call" | custom-call | tf_op jit(solution)/shard_map/layer/pallas_call | solution.py:1150
  291.9 0.0 copy-start
  291.9 0.9 fusion.5
  292.8 0.6 convert_divide_fusion
  293.3 1.0 broadcast_multiply_fusion
  294.4 0.7 fusion.4
  295.1 0.7 slice.28
  295.8 1.0 bitcast_multiply_fusion
  296.9 0.7 copy.30
  297.6 0.4 copy-done.2
  297.9 0.7 copy.31
  298.6 0.7 copy.32
  299.3 0.8 copy.33
  (14 shorter events, 0.0 us)
Async XLA Ops:
  1.3 0.7 copy-start.11
  1.3 0.7 copy-start.9
  1.3 0.7 copy-start.10
  1.3 1.3 copy-start.7
  1.3 1.3 copy-start.8
  4.6 0.9 copy-start.4
  4.6 1.0 copy-start.5
  291.9 4.0 %copy-start = (f32[2,144,768]{2,1,0:T(8,128)S(1)}, f32[2,144,768]{2,1,0:T(8,128)}, u32[]{:S(2)}) copy-start(f32[2,144,768]{2,1,0:T(8,128)} %get-tuple-element.23) | copy-start | bytes 2654212
  295.8 1.0 copy-start.3
  296.9 1.1 copy-start.2
  296.9 1.8 copy-start.6
  297.9 1.4 copy-start.1

commit v2 on v1

--- a/solution.py
+++ b/solution.py
@@ -430,7 +430,7 @@
         self.recvs += count
         return first
 
-    def send(self, src, dst, slot, device, is_self=None):
+    def send(self, src, dst, slot, device, is_self=None, only=None):
         mine = self.sends
         self.sends += 1
         remote = pltpu.make_async_remote_copy(
@@ -441,7 +441,18 @@
             device_id=device,
             device_id_type=MESH,
         )
-        if is_self is None:
+        if only is not None:
+
+            @pl.when(only)
+            def _():
+                remote.start()
+
+            def finish():
+                @pl.when(only)
+                def _():
+                    remote.wait_send()
+
+        elif is_self is None:
             remote.start()
             finish = remote.wait_send
         else:
@@ -479,16 +490,16 @@
         self.pending = []
 
 
-N_SEM = 224
+N_SEM = 256
 
 
 def layer_kernel(
-    tok, cot, cs, bias, wqkv, wo, wgu, wdt,
-    o_out, o_ing, o_gain, o_qkv, o_o, o_gu, o_dt,
-    csf, b2, x2, wqz, woz, wq, wok, wg8, wd8, c8, n8, n1, qf, kvf, kv, q6, p6, o6, ab,
+    tok, cot, cs, bias, gain, wqkv, wo, wgate, wup, wdt,
+    o_out, o_ing, o_gain, o_q, o_k, o_v, o_o, o_gate, o_up, o_d,
+    csf, b2, x2, gb, grow, wqz, woz, wq, wok, wg8, wd8, c8, n8, n1, qf, kvf, kv, q6, p6, o6, ab,
     mp, ml, mid, dmid, dmb, dm4, do6, act, pt, l1, s2, l2, l1o, s2o, l2o,
-    ggu, lgu, sgu, lf, gdt, lgd, sgd, ld, lo, lq, so, sq, lzo, lzq, dkv, lx, sx, lkz,
-    lg, sg, lgz, dqk, send_sems, recv_sems,
+    ggu, lgu, lf, gdt, lgd, sgd, ld, lo, lq, lk, so, sq, sk, lzo, lzq, lzk, kvg, dkv, lx, sx, lkz,
+    lg, sg, dqk, send_sems, recv_sems,
 ):
     net = Wires(send_sems, recv_sems)
     dp = lax.axis_index("dp")
@@ -543,96 +554,162 @@
     net.send(tok, x2, r_tok, partner)
     net.send(cs, csf.at[pl.ds(tokens, tokens)], r_tok + 1, partner)
     net.send(bias, b2.at[1], r_tok + 2, partner)
-    r_wqz, r_woz = net.slots(4), net.slots(4)
-    r_wq, r_wo = net.slots(16), net.slots(16)
+    r_g = net.slots(8)
+    r_wqz, r_wq = net.slots(4), net.slots(16)
 
     def spread_qkv(k, src):
         zs = zat(k)
-        for hx in range(2):
-            for hy in range(2):
-                net.send(
-                    src,
-                    wq.at[c, pl.ds(off(2 * zs + x, rows), rows)],
-                    r_wq + k * 4 + hx * 2 + c,
-                    dev(flip(y, hy), y, z, flip(x, hx)),
-                    is_self=(c == y) if hx + hy == 0 else None,
-                )
-
-    def spread_wo(k, src):
-        zs = zat(k)
-        core = zs // 2
-        for hx in range(2):
-            for hy in range(2):
-                net.send(
-                    src,
-                    wok.at[dp, pl.ds(off(2 * lax.rem(zs, 2) + x, rows), rows)],
-                    r_wo + lax.rem(zs, 2) * 8 + hx * 4 + hy * 2 + c,
-                    dev(flip(y, hy), core, z, flip(x, hx)),
-                    is_self=(c == core) if hx + hy == 0 else None,
-                )
+        for hx, hy in ((0, 0), (1, 0), (0, 1)):
+            net.send(
+                src,
+                wq.at[c, pl.ds(off(2 * zs + x, rows), rows)],
+                r_wq + k * 4 + hx * 2 + c,
+                dev(flip(y, hy), y, z, flip(x, hx)),
+                is_self=(c == y) if hx + hy == 0 else None,
+            )
 
     for k in range(1, 4):
         net.send(wqkv, wqz.at[k - 1], r_wqz + k, dev(y, c, zat(k), x))
     spread_qkv(0, wqkv)
-    for k in range(1, 4):
-        net.send(wo, woz.at[k - 1], r_woz + k, dev(y, c, zat(k), x))
+    for k in range(4):
+        for hx in range(2):
+            if k + hx:
+                net.send(gain, gb.at[ctx], r_g + 2 * k + hx, dev(y, c, zat(k), flip(x, hx)))
 
     csf[0:tokens] = cs[...]
     b2[0] = bias[...]
+    gb[ctx] = gain[...]
+    c8[0] = cot[...]
 
     def normed(values):
         v = values.astype(F32)
         inv = lax.rsqrt(jnp.mean(v * v, -1, keepdims=True) + EPSILON)
         return v * inv, inv
 
-    n1[0:tokens] = normed(tok[...])[0].astype(BF16)
-    net.recv(x2, r_tok)
-    n1[tokens : 2 * tokens] = normed(x2[...])[0].astype(BF16)
-    net.recv(csf.at[pl.ds(tokens, tokens)], r_tok + 1)
-    net.recv(b2.at[1], r_tok + 2)
-
     for k in range(1, 4):
         net.recv(wqz.at[k - 1], r_wqz + k)
         spread_qkv(k, wqz.at[k - 1])
 
-    r_gu, r_wd = net.slots(8), net.slots(4)
+    r_woz, r_wo = net.slots(4), net.slots(16)
+
+    def spread_wo(k, src):
+        zs = zat(k)
+        core = zs // 2
+        for hx, hy in ((0, 0), (1, 0), (0, 1)):
+            net.send(
+                src,
+                wok.at[dp, pl.ds(off(2 * lax.rem(zs, 2) + x, rows), rows)],
+                r_wo + lax.rem(zs, 2) * 8 + hx * 4 + hy * 2 + c,
+                dev(flip(y, hy), core, z, flip(x, hx)),
+                is_self=(c == core) if hx + hy == 0 else None,
+            )
+
+    r_gu, r_wd, r_wy = net.slots(16), net.slots(2), net.slots(2)
+    home = y_c == z_lo
+
+    def send_ff(m):
+        for zh in range(2):
+            for hx in range(2):
+                net.send(
+                    (wgate, wup)[m].at[:, pl.ds(off(flip(x, hx), ff), ff)],
+                    wg8.at[m, pl.ds(off(ctx, rows), rows)],
+                    r_gu + m * 8 + ctx,
+                    dev(y, c, 2 * zh + y_c, flip(x, hx)),
+                    is_self=(z == 2 * zh + y_c) if hx == 0 else None,
+                )
+
+    ff_passed = []
+
+    def pass_ff(m):
+        for i in range(n_ctx):
+            part = wg8.at[m, pl.ds(rows * i, rows)]
+
+            @pl.when(home)
+            def _():
+                net.recv(part, r_gu + m * 8 + i)
+
+            ff_passed.append(
+                net.send(part, part, r_gu + m * 8 + i, dev(1 - y, c, z, x), only=home)
+            )
+
+    def take_ff(m):
+        for i in range(n_ctx):
+
+            @pl.when(jnp.logical_not(home))
+            def _():
+                net.recv(wg8.at[m, pl.ds(rows * i, rows)], r_gu + m * 8 + i)
+
+    def send_down():
+        z_x = z_hi + z_lo - 2 * z_hi * z_lo
+        for zh in range(2):
+            net.send(
+                wdt,
+                wd8.at[pl.ds(off(dp, drows), drows)],
+                r_wd + c,
+                dev(y, z_lo, 2 * zh + z_x, x),
+                is_self=jnp.logical_and(z == 2 * zh + z_x, c == z_lo),
+            )
+
+    for k in range(1, 4):
+        net.send(wo, woz.at[k - 1], r_woz + k, dev(y, c, zat(k), x))
+    spread_wo(0, wo)
+    send_ff(0)
+
     for k in range(4):
         for hx in range(2):
-            net.send(
-                wgu.at[:, :, pl.ds(off(flip(x, hx), ff), ff)],
-                wg8.at[:, pl.ds(off(ctx, rows), rows)],
-                r_gu + k * 2 + hx,
-                dev(y_c, c, zat(k), flip(x, hx)),
-                is_self=(c == 0) if k + hx == 0 else None,
-            )
-    wd_c = z_lo
-    wd_y = z_hi + wd_c - 2 * z_hi * wd_c
-    wd_home = jnp.logical_and(wd_c == c, wd_y == y)
+            if k + hx:
+                net.recv(gb.at[2 * zat(k) + flip(x, hx)], r_g + 2 * k + hx)
+    for t in range(n_ctx):
+        grow[:, rows * t : rows * (t + 1)] = gb[t]
+    n1[0:tokens] = (normed(tok[...])[0] * grow[0:1]).astype(BF16)
+    net.recv(x2, r_tok)
+    n1[tokens : 2 * tokens] = (normed(x2[...])[0] * grow[0:1]).astype(BF16)
+    net.recv(csf.at[pl.ds(tokens, tokens)], r_tok + 1)
+    net.recv(b2.at[1], r_tok + 2)
+
     for k in range(4):
-        net.send(
-            wdt,
-            wd8.at[pl.ds(off(dp, drows), drows)],
-            r_wd + dp,
-            dev(wd_y, wd_c, zat(k), x),
-            is_self=wd_home if k == 0 else None,
-        )
-    spread_wo(0, wo)
+        at_x = pl.ds(off(2 * zat(k) + x, rows), rows)
+        at_o = pl.ds(off(2 * zat(k) + 1 - x, rows), rows)
+        slot = r_wq + k * 4
+
+        @pl.when(c == y)
+        def _():
+            net.recv(wq.at[0, at_o], slot + 2)
+
+        net.send(wq.at[0, at_o], wq.at[0, at_o], slot + 2, dev(1 - y, c, z, x), only=(c == y))
+
+        @pl.when(c != y)
+        def _():
+            net.recv(wq.at[1, at_x], slot + 1)
+
+        net.send(wq.at[1, at_x], wq.at[1, at_x], slot + 3, dev(y, c, z, 1 - x), only=(c != y))
     for k in range(1, 4):
         net.recv(woz.at[k - 1], r_woz + k)
         spread_wo(k, woz.at[k - 1])
+    for k in range(4):
+        at_x = pl.ds(off(2 * zat(k) + x, rows), rows)
+        at_o = pl.ds(off(2 * zat(k) + 1 - x, rows), rows)
+        slot = r_wq + k * 4
+
+        @pl.when(c == y)
+        def _():
+            net.recv(wq.at[1, at_x], slot + 1)
+
+        @pl.when(c != y)
+        def _():
+            net.recv(wq.at[0, at_o], slot + 2)
+
+        net.recv(wq.at[0, at_x], slot)
+        net.recv(wq.at[1, at_o], slot + 3)
 
     def gather_start(buf, slot):
+        net.send(buf.at[0], buf.at[1], slot + 4, partner)
         for h in range(1, 4):
-            net.send(buf.at[0], buf.at[2 * h], slot + h, dev(flip(y, h % 2), c, z, flip(x, h // 2)))
-        net.send(buf.at[0], buf.at[1], slot + 4, partner)
+            net.send(buf.at[0], buf.at[2 * h], slot + h, dev(y, c, zat(h % 2), flip(x, h // 2)))
 
     def gather_pass(buf, slot, h):
         net.recv(buf.at[2 * h], slot + h)
         net.send(buf.at[2 * h], buf.at[2 * h + 1], slot + 4 + h, partner)
-
-    c8[0] = cot[...]
-    r_c8 = net.slots(8)
-    gather_start(c8, r_c8)
 
     lane = lax.broadcasted_iota(jnp.int32, (2 * tokens, 128), 1)
     low_half = lax.rem(lane, HEAD_SIZE) < HEAD_SIZE // 2
@@ -642,21 +719,12 @@
         turned = other * csf[:, 128:256]
         return tile * csf[:, 0:128] + (turned if forward else -turned)
 
-    for k in range(4):
-        for hx in range(2):
-            for cc in range(2):
-                net.recv(
-                    wq.at[cc, pl.ds(off(2 * zat(k) + flip(x, hx), rows), rows)],
-                    r_wq + k * 4 + hx * 2 + cc,
-                )
     qf[:, qw:] = jnp.zeros((2 * tokens, qf.shape[1] - qw), F32)
     for part in range(2):
         got = dot_nn(n1[...], wq[part])
         qf[:, qcols * part : qcols * (part + 1)] = got[:, :qcols]
         kvf[:, kcols * part : kcols * (part + 1)] = got[:, qcols : qcols + kcols]
         kvf[:, kw + kcols * part : kw + kcols * (part + 1)] = got[:, qcols + kcols :]
-    for t in range(qf.shape[1] // 128):
-        qf[:, 128 * t : 128 * (t + 1)] = turn(qf[:, 128 * t : 128 * (t + 1)], True) * scale
 
     def turn_keys(forward):
         for t in range(kw // 128 + 1):
@@ -673,17 +741,30 @@
     for k in range(1, 4):
         net.send(kv.at[:, own_keys], kv.at[:, own_keys], r_kz + k, dev(y, c, zat(k), x))
     net.send(kv.at[:, own_keys], kv.at[:, own_keys], r_kx, dev(y, c, z, 1 - x))
+    send_ff(1)
+    send_down()
+
+    for t in range(qf.shape[1] // 128):
+        qf[:, 128 * t : 128 * (t + 1)] = turn(qf[:, 128 * t : 128 * (t + 1)], True) * scale
     for s in range(2):
         for h in range(heads):
             q6[s * groups + h // per, (h % per) * tokens : (h % per + 1) * tokens] = qf[
                 s * tokens : (s + 1) * tokens, HEAD_SIZE * h : HEAD_SIZE * (h + 1)
             ].astype(BF16)
-    for h in range(1, 4):
-        gather_pass(c8, r_c8, h)
     for k in range(1, 4):
         part = pl.ds(off(2 * zat(k) + x, tokens), tokens)
         net.recv(kv.at[:, part], r_kz + k)
         net.send(kv.at[:, part], kv.at[:, part], r_kx + k, dev(y, c, z, 1 - x))
+    r_c8 = net.slots(8)
+    gather_start(c8, r_c8)
+    for zz in range(2):
+        part = wok.at[2 * (1 - y), pl.ds(off(2 * zz + x, rows), rows)]
+        net.recv(part, r_wo + zz * 8 + 2)
+        net.send(part, part, r_wo + zz * 8 + 6, dev(y, c, z, 1 - x))
+        part = wok.at[2 * y + 1, pl.ds(off(2 * zz + 1 - x, rows), rows)]
+        net.recv(part, r_wo + zz * 8 + 5)
+        net.send(part, part, r_wo + zz * 8 + 7, dev(1 - y, c, z, x))
+    pass_ff(0)
     for k in range(4):
         net.recv(kv.at[:, pl.ds(off(2 * zat(k) + 1 - x, tokens), tokens)], r_kx + k)
 
@@ -707,47 +788,43 @@
 
     lax.fori_loop(0, 2, attend, 0)
 
-    for zz in range(2):
-        for hx in range(2):
-            for hy in range(2):
-                for cc in range(2):
-                    part = 2 * flip(y, hy) + cc
-                    net.recv(
-                        wok.at[part, pl.ds(off(2 * zz + flip(x, hx), rows), rows)],
-                        r_wo + zz * 8 + hx * 4 + hy * 2 + cc,
-                    )
+    for hx, hy, cc in ((0, 0, 0), (0, 0, 1), (0, 1, 1), (1, 0, 0), (1, 1, 0), (1, 1, 1)):
+        for zz in range(2):
+            net.recv(
+                wok.at[2 * flip(y, hy) + cc, pl.ds(off(2 * zz + flip(x, hx), rows), rows)],
+                r_wo + zz * 8 + hx * 4 + hy * 2 + cc,
+            )
     for part in range(4):
         got = dot_nn(ab[:, 0:qw], wok[part])
         for s in range(2):
             mp[s, :, qcols * part : qcols * (part + 1)] = got[s * tokens : (s + 1) * tokens]
     r_ml = net.slots(1)
     mp_sent = net.send(mp.at[1], ml, r_ml, partner)
+    pass_ff(1)
+    for cc in range(2):
+        part = wd8.at[pl.ds(off(2 * y + cc, drows), drows)]
+        net.recv(part, r_wd + cc)
+        net.send(part, part, r_wy + cc, dev(1 - y, c, z, x))
+    for h in range(1, 4):
+        gather_pass(c8, r_c8, h)
     net.recv(ml, r_ml)
     mid[...] = tok[...].astype(F32) + mp[0] + ml[...]
-    n8[0] = normed(mid[...])[0].astype(BF16)
+    n8[0] = (normed(mid[...])[0] * grow[1:2]).astype(BF16)
     r_n8 = net.slots(8)
     gather_start(n8, r_n8)
 
+    net.recv(c8.at[1], r_c8 + 4)
     for h in range(1, 4):
         net.recv(c8.at[2 * h + 1], r_c8 + 4 + h)
-    net.recv(c8.at[1], r_c8 + 4)
-    for k in range(4):
-        for hx in range(2):
-            net.recv(
-                wg8.at[:, pl.ds(off(2 * zat(k) + flip(x, hx), rows), rows)], r_gu + k * 2 + hx
-            )
-    for part in range(4):
-        net.recv(wd8.at[pl.ds(drows * part, drows)], r_wd + part)
-    for h in range(1, 4):
-        gather_pass(n8, r_n8, h)
-    net.recv(n8.at[1], r_n8 + 4)
-    for h in range(1, 4):
-        net.recv(n8.at[2 * h + 1], r_n8 + 4 + h)
+    take_ff(0)
+    take_ff(1)
+    for cc in range(2):
+        net.recv(wd8.at[pl.ds(off(2 * (1 - y) + cc, drows), drows)], r_wy + cc)
 
     all_tokens = 8 * tokens
 
-    def feed(i, carry):
-        pair = pl.ds(2 * i, 2)
+    def feed(i):
+        pair = slice(2 * i, 2 * i + 2)
         here = n8[pair].reshape(2 * tokens, width)
         grad_inner = dot_nn(c8[pair].reshape(2 * tokens, width), wd8[...])
         gate = dot_nn(here, wg8[0])
@@ -756,26 +833,24 @@
         silu = gate * sig
         dgate = (grad_inner * up * sig * (1.0 + gate * (1.0 - sig))).astype(BF16)
         dup = (grad_inner * silu).astype(BF16)
-        at = off(i, 2 * tokens)
-        act[pl.ds(at, 2 * tokens)] = (silu * up).astype(BF16)
-        act[pl.ds(at + all_tokens, 2 * tokens)] = dgate
-        act[pl.ds(at + 2 * all_tokens, 2 * tokens)] = dup
+        at = 2 * tokens * i
+        act[at : at + 2 * tokens] = (silu * up).astype(BF16)
+        act[at + all_tokens : at + all_tokens + 2 * tokens] = dgate
+        act[at + 2 * all_tokens : at + 2 * all_tokens + 2 * tokens] = dup
         pt[pair] = (dot_nt(dgate, wg8[0]) + dot_nt(dup, wg8[1])).astype(BF16).reshape(2, tokens, width)
-        return carry
-
-    lax.fori_loop(0, 4, feed, 0)
-
-    def reduce_start(part, land, slot):
-        return [net.send(part.at[2 * h + 1], land.at[h], slot + h, partner) for h in range(4)]
-
-    def reduce_pass(part, land, out, land2, slot):
-        for h in range(1, 4):
-            net.recv(land.at[h], slot + h)
-            out[h - 1] = (part[2 * h].astype(F32) + land[h].astype(F32)).astype(BF16)
-            net.send(
-                out.at[h - 1], land2.at[h - 1], slot + 4 + h,
-                dev(flip(y, h % 2), c, z, flip(x, h // 2)),
-            )
+
+    def reduce_start(part, land, slot, h):
+        return net.send(part.at[2 * h + 1], land.at[h], slot + h, partner)
+
+    def reduce_pass(part, land, out, land2, slot, h):
+        net.recv(land.at[h], slot + h)
+        out[h - 1] = (part[2 * h].astype(F32) + land[h].astype(F32)).astype(BF16)
+        net.send(
+            out.at[h - 1], land2.at[h - 1], slot + 4 + h,
+            dev(y, c, zat(h % 2), flip(x, h // 2)),
+        )
+
+    def reduce_own(part, land, slot):
         net.recv(land.at[0], slot)
         return part[0].astype(F32) + land[0].astype(F32)
 
@@ -786,6 +861,20 @@
             total = total + land2[h - 1].astype(F32)
         return total
 
+    r_dn = net.slots(8)
+    pt_sent = []
+    net.recv(n8.at[1], r_n8 + 4)
+    for h in range(4):
+        if h:
+            gather_pass(n8, r_n8, h)
+            net.recv(n8.at[2 * h + 1], r_n8 + 4 + h)
+        feed(h)
+        pt_sent.append(reduce_start(pt, l1, r_dn, h))
+        if h > 1:
+            reduce_pass(pt, l1, s2, l2, r_dn, h - 1)
+    reduce_pass(pt, l1, s2, l2, r_dn, 3)
+    dmid[...] = reduce_own(pt, l1, r_dn)
+
     def flat(ref, i):
         return ref[:, :, pl.ds(off(i, 128), 128)].reshape(all_tokens, 128)
 
@@ -805,50 +894,43 @@
         pt[pl.ds(2 * i, 2)] = got.astype(BF16).reshape(2, tokens, width)
         return carry
 
-    r_dn = net.slots(8)
-    pt_sent = reduce_start(pt, l1, r_dn)
+    r_gd, r_gz = net.slots(1), net.slots(4)
+    half = 2 * drows
     lax.fori_loop(0, width // 128, grad_d, 0)
-    dmid[...] = reduce_pass(pt, l1, s2, l2, r_dn)
-
-    gd_z = 2 * y_c + c
-    r_gd = net.slots(4)
-
-    def to_home(k):
-        return pltpu.make_async_remote_copy(
-            src_ref=gdt, dst_ref=lgd.at[k - 1],
-            send_sem=send_sems.at[N_SEM - 4 + k], recv_sem=recv_sems.at[r_gd + k],
-            device_id=dev(y, c, zat(k), x), device_id_type=MESH,
-        )
-
-    for k in range(1, 4):
-        @pl.when(zat(k) == gd_z)
-        def _(k=k):
-            to_home(k).start()
-
+    net.send(gdt.at[pl.ds(off(1 - y, half), half)], lgd, r_gd, dev(1 - y, c, z, x))
     lax.fori_loop(0, width // 128, grad_gu, 0)
-    r_gz = net.slots(4)
-    for k in range(1, 4):
+    for zt in range(4):
+        at = pl.ds(2 * rows * zt, 2 * rows)
         net.send(
-            ggu.at[:, pl.ds(off(zat(k), 2 * rows), 2 * rows)], lgu.at[k - 1], r_gz + k,
-            dev(y, c, zat(k), x),
+            ggu.at[:, at], lgu.at[:, at], r_gz + zt, dev(1 - y, c, z, x),
+            only=jnp.logical_not(home),
         )
     for finish in pt_sent:
         net.done(finish)
     lax.fori_loop(0, 4, feed_out, 0)
     r_out = net.slots(8)
-    reduce_start(pt, l1o, r_out)
+    for h in range(4):
+        reduce_start(pt, l1o, r_out, h)
 
     total = dmid[...] + reduce_end(l2, r_dn)
     normed_two, inv_two = normed(mid[...])
-    sg[0] = jnp.zeros(sg.shape[1:], F32)
-    sg[0, 1:2] = jnp.sum(total * normed_two, 0, keepdims=True)
+    total = total * grow[1:2]
     dmid[...] = cot[...].astype(F32) + inv_two * (
         total - normed_two * jnp.mean(total * normed_two, -1, keepdims=True)
     )
     dmb[0] = dmid[...].astype(BF16)
     r_dm = net.slots(1)
     net.send(dmb.at[0], dmb.at[1], r_dm, partner)
-    mid[...] = mid[...] + reduce_pass(pt, l1o, s2o, l2o, r_out)
+
+    r_ld = net.slots(2)
+    net.recv(lgd, r_gd)
+    sgd[...] = (gdt[pl.ds(off(y, half), half)].astype(F32) + lgd[...].astype(F32)).astype(BF16)
+    gd_z = 2 * (z_lo + c - 2 * z_lo * c) + c
+    for cc in range(2):
+        net.send(
+            sgd.at[pl.ds(cc * drows, drows)], ld.at[z_hi], r_ld + z_hi, dev(y, cc, gd_z, x),
+            is_self=jnp.logical_and(z == gd_z, c == cc),
+        )
     net.recv(dmb.at[1], r_dm)
 
     for part in range(4):
@@ -882,7 +964,7 @@
                     else:
                         net.send(src, dst, slot, dev(flip(y, hy), flip(c, hc), z, flip(x, hx)))
 
-    def attend_back(s, carry):
+    def attend_back(s):
         for g in range(groups):
             at = s * groups + g
             kg = kv[s, :, HEAD_SIZE * g : HEAD_SIZE * (g + 1)]
@@ -900,63 +982,71 @@
                 dkv[t, s, kw + HEAD_SIZE * g : kw + HEAD_SIZE * (g + 1)] = dvals[:, cols].astype(BF16)
             for i in range(per):
                 h = g * per + i
-                qf[pl.ds(off(s, tokens), tokens), HEAD_SIZE * h : HEAD_SIZE * (h + 1)] = dquery[
+                qf[s * tokens : (s + 1) * tokens, HEAD_SIZE * h : HEAD_SIZE * (h + 1)] = dquery[
                     i * tokens : (i + 1) * tokens
                 ]
-        return carry
-
-    lax.fori_loop(0, 2, attend_back, 0)
+
+    attend_back(0)
+    r_gf = net.slots(4)
+    for k in (3, 2, 1, 0):
+        at = pl.ds(off(zat(k), 2 * rows), 2 * rows)
+
+        @pl.when(home)
+        def _():
+            net.recv(lgu.at[:, at], r_gz + zat(k))
+            ggu[:, at] = (ggu[:, at].astype(F32) + lgu[:, at].astype(F32)).astype(BF16)
+
+        for hx in range(2):
+            src = ggu.at[:, pl.ds(off(2 * zat(k) + flip(x, hx), rows), rows)]
+            dst = lf.at[x, z_hi]
+            slot = r_gf + x * 2 + z_hi
+            if k + hx:
+                net.send(src, dst, slot, dev(y, c, zat(k), flip(x, hx)), only=home)
+            else:
+
+                @pl.when(home)
+                def _():
+                    net.keep(src, dst, slot)
+
+    attend_back(1)
     r_dx, r_dz = net.slots(4), net.slots(4)
-    for k in range(4):
+    for k in (1, 2, 3, 0):
         net.send(dkv.at[2 * zat(k) + 1 - x], lx.at[k], r_dx + k, dev(y, c, z, 1 - x))
     for t in range(qf.shape[1] // 128):
         qf[:, 128 * t : 128 * (t + 1)] = turn(qf[:, 128 * t : 128 * (t + 1)], False)
     for part in range(2):
         dqk[part, :, 0:qcols] = qf[:, qcols * part : qcols * (part + 1)].astype(BF16)
+        got = dot_tn(n1[...], dqk[part, :, 0:qcols]).astype(BF16)
+        for t in range(n_ctx):
+            p6[t // 2, (t % 2) * rows : (t % 2 + 1) * rows, ff * part : ff * part + qcols] = got[
+                rows * t : rows * (t + 1)
+            ]
+
+    def send_grads(source, land, slot):
+        for k in (3, 2, 1, 0):
+            for hx in range(2):
+                for ct in range(2):
+                    net.send(
+                        source(zat(k), flip(x, hx), ct),
+                        land.at[k, hx * 2 + y_c],
+                        slot + k * 4 + hx * 2 + y_c,
+                        dev(c, ct, z, flip(x, hx)),
+                        is_self=jnp.logical_and(y == c, c == ct) if hx == 0 else None,
+                    )
+
     for k in range(1, 4):
         net.recv(lx.at[k], r_dx + k)
         sx[k - 1] = (dkv[2 * zat(k) + x].astype(F32) + lx[k].astype(F32)).astype(BF16)
         net.send(sx.at[k - 1], lkz.at[k - 1], r_dz + k, dev(y, c, zat(k), x))
-
-    r_gf, r_ld = net.slots(2), net.slots(1)
-    mine = ggu[:, pl.ds(off(z, 2 * rows), 2 * rows)].astype(F32)
-    for k in range(1, 4):
-        net.recv(lgu.at[k - 1], r_gz + k)
-        mine = mine + lgu[k - 1].astype(F32)
-    sgu[...] = mine.astype(BF16)
-    for hx in range(2):
-        net.send(
-            sgu.at[:, pl.ds(off(flip(x, hx), rows), rows)], lf.at[hx], r_gf + hx,
-            dev(y_c, c, z, flip(x, hx)), is_self=(c == 0) if hx == 0 else None,
-        )
-
-    def share(hy, hc):
-        to_dp = 2 * flip(y, hy) + flip(c, hc)
-        return pltpu.make_async_remote_copy(
-            src_ref=sgd.at[pl.ds(off(to_dp, drows), drows)], dst_ref=ld,
-            send_sem=send_sems.at[N_SEM - 8 + 2 * hy + hc], recv_sem=recv_sems.at[r_ld],
-            device_id=dev(flip(y, hy), flip(c, hc), z, x), device_id_type=MESH,
-        )
-
-    @pl.when(z == gd_z)
-    def _():
-        for k in range(1, 4):
-            net.recv(lgd.at[k - 1], r_gd + k)
-
-        def add(i, carry):
-            at = pl.ds(off(i, 128), 128)
-            part = gdt[at].astype(F32)
-            for k in range(3):
-                part = part + lgd[k, at].astype(F32)
-            sgd[at] = part.astype(BF16)
-            return carry
-
-        lax.fori_loop(0, width // 128, add, 0)
-        net.keep(sgd.at[pl.ds(off(dp, drows), drows)], ld, r_ld)
-        for hy, hc in ((0, 1), (1, 0), (1, 1)):
-            share(hy, hc).start()
-
-    def attn_pass(land, out, send_at, slot, absolute):
+    r_gq = net.slots(16)
+    send_grads(
+        lambda zt, xt, ct: p6.at[zt, pl.ds(off(xt, rows), rows), pl.ds(ff * ct, ff)], lq, r_gq
+    )
+    for h in range(1, 4):
+        reduce_pass(pt, l1o, s2o, l2o, r_out, h)
+    mid[...] = mid[...] + reduce_own(pt, l1o, r_out)
+
+    def attn_pass(land, out, staged, arrived, send_slot, slot, absolute):
         for k in (1, 2, 3, 0):
             at = zat(k) if absolute else k
             part = 0.0
@@ -966,11 +1056,16 @@
             if k == 0:
                 out[...] = part
             else:
-                send_at[0][k - 1] = part.astype(BF16)
-                net.send(send_at[0].at[k - 1], send_at[1].at[k - 1], send_at[2] + k, dev(y, c, zat(k), x))
-
-    r_zo, r_zq = net.slots(4), net.slots(4)
-    attn_pass(lo, o_o, (so, lzo, r_zo), r_go, True)
+                staged[k - 1] = part.astype(BF16)
+                net.send(staged.at[k - 1], arrived.at[k - 1], send_slot + k, dev(y, c, zat(k), x))
+
+    def attn_end(out, arrived, slot):
+        for k in range(1, 4):
+            net.recv(arrived.at[k - 1], slot + k)
+            out[...] = out[...] + arrived[k - 1].astype(F32)
+
+    r_zo, r_zq, r_zk = net.slots(4), net.slots(4), net.slots(4)
+    attn_pass(lo, o_o, so, lzo, r_zo, r_go, True)
 
     net.recv(lx.at[0], r_dx)
     total = dkv[2 * z + x].astype(F32) + lx[0].astype(F32)
@@ -983,84 +1078,68 @@
     for part in range(2):
         dqk[part, :, qcols : qcols + kcols] = kvf[:, kcols * part : kcols * (part + 1)].astype(BF16)
         dqk[part, :, qcols + kcols :] = kvf[:, kw + kcols * part : kw + kcols * (part + 1)].astype(BF16)
+    for finish in ff_passed:
+        net.done(finish)
     for part in range(2):
-        got = dot_tn(n1[...], dqk[part]).astype(BF16)
-        for t in range(n_ctx):
-            p6[t // 2, (t % 2) * rows : (t % 2 + 1) * rows, 512 * part : 512 * part + qcols + 2 * kcols] = got[
-                rows * t : rows * (t + 1)
-            ]
-    r_gq = net.slots(16)
-    hy_c = y_c
-    for k in (1, 2, 3, 0):
-        for hx in range(2):
-            for ct in range(2):
-                net.send(
-                    p6.at[zat(k), pl.ds(off(flip(x, hx), rows), rows), pl.ds(512 * ct, 512)],
-                    lq.at[k, hx * 2 + hy_c],
-                    r_gq + k * 4 + hx * 2 + hy_c,
-                    dev(c, ct, z, flip(x, hx)),
-                    is_self=jnp.logical_and(y == c, c == ct) if hx == 0 else None,
-                )
+        wg8[part, :, 0 : 2 * kcols] = dot_tn(n1[...], dqk[part, :, qcols:]).astype(BF16)
+    r_gk = net.slots(16)
+    send_grads(
+        lambda zt, xt, ct: wg8.at[ct, pl.ds(off(2 * zt + xt, rows), rows), pl.ds(0, 256)], lk, r_gk
+    )
     net.done(mp_sent)
     got = dot_nt(dqk[0], wq[0]) + dot_nt(dqk[1], wq[1])
     for s in range(2):
         mp[s] = got[s * tokens : (s + 1) * tokens]
     r_dn1 = net.slots(1)
     net.send(mp.at[1], ml, r_dn1, partner)
+    attn_pass(lq, o_q, sq, lzq, r_zq, r_gq, False)
     net.recv(ml, r_dn1)
     total = mp[0] + ml[...]
     normed_one, inv_one = normed(tok[...])
-    sg[0, 0:1] = jnp.sum(total * normed_one, 0, keepdims=True)
-    r_lg = net.slots(8)
-    for h in range(1, 8):
-        net.send(
-            sg.at[0], lg.at[h], r_lg + h, dev(flip(y, (h // 2) % 2), flip(c, h % 2), z, flip(x, h // 4))
-        )
+    total = total * grow[0:1]
     o_ing[...] = (
         dmid[...]
         + inv_one * (total - normed_one * jnp.mean(total * normed_one, -1, keepdims=True))
     ).astype(BF16)
-    gains = sg[0]
-    for h in range(1, 8):
-        net.recv(lg.at[h], r_lg + h)
-        gains = gains + lg[h]
-    sg[1] = gains
-    r_lgz = net.slots(4)
-    for k in range(1, 4):
-        net.send(sg.at[1], lgz.at[k - 1], r_lgz + k, dev(y, c, zat(k), x))
-
-    attn_pass(lq, o_qkv, (sq, lzq, r_zq), r_gq, False)
+    attn_pass(lk, kvg, sk, lzk, r_zk, r_gk, False)
 
     o_out[...] = (mid[...] + reduce_end(l2o, r_out)).astype(BF16)
-    for hx in range(2):
-        net.recv(lf.at[hx], r_gf + hx)
-        o_gu[:, :, pl.ds(off(flip(x, hx), ff), ff)] = lf[hx].astype(F32)
-    net.recv(ld, r_ld)
-    o_dt[...] = ld[...].astype(F32)
-    for out, land, slot in ((o_o, lzo, r_zo), (o_qkv, lzq, r_zq)):
-        for k in range(1, 4):
-            net.recv(land.at[k - 1], slot + k)
-            out[...] = out[...] + land[k - 1].astype(F32)
-    gains = sg[1]
-    for k in range(1, 4):
-        net.recv(lgz.at[k - 1], r_lgz + k)
-        gains = gains + lgz[k - 1]
-    o_gain[...] = gains
-
-    for k in range(1, 4):
-        @pl.when(zat(k) == gd_z)
-        def _(k=k):
-            to_home(k).wait_send()
-
-    @pl.when(z == gd_z)
-    def _():
-        for hy, hc in ((0, 1), (1, 0), (1, 1)):
-            share(hy, hc).wait_send()
-
+    gains = [0.0, 0.0]
+    for h in range(2):
+        for zh in range(2):
+            net.recv(lf.at[h, zh], r_gf + h * 2 + zh)
+        for m in range(2):
+            got = lf[h, 0, m].astype(F32) + lf[h, 1, m].astype(F32)
+            cols = slice(h * ff, (h + 1) * ff)
+            (o_gate, o_up)[m][:, cols] = got
+            gains[1] = gains[1] + jnp.sum(
+                got * (wgate, wup)[m][:, cols].astype(F32), 1, keepdims=True
+            )
+    for zh in range(2):
+        net.recv(ld.at[zh], r_ld + zh)
+    o_d[...] = (ld[0].astype(F32) + ld[1].astype(F32)).T
+    attn_end(o_o, lzo, r_zo)
+    attn_end(o_q, lzq, r_zq)
+    gains[0] = jnp.sum(o_q[...] * wqkv[:, 0:qcols].astype(F32), 1, keepdims=True)
+    attn_end(kvg, lzk, r_zk)
+    gains[0] = gains[0] + jnp.sum(kvg[...] * wqkv[:, qcols:].astype(F32), 1, keepdims=True)
+    o_k[...] = kvg[:, 0:kcols]
+    o_v[...] = kvg[:, kcols:]
+    column = lax.broadcasted_iota(jnp.int32, (rows, 128), 1)
+    both = jnp.where(column == 0, gains[0], jnp.where(column == 1, gains[1], 0.0))
+    sg[...] = both.T[0:8]
+    r_lg = net.slots(4)
+    for h in range(1, 4):
+        net.send(sg, lg.at[h - 1], r_lg + h, dev(flip(y, h // 2), flip(c, h % 2), z, x))
+    total = sg[...]
+    for h in range(1, 4):
+        net.recv(lg.at[h - 1], r_lg + h)
+        total = total + lg[h - 1]
+    o_gain[...] = total / gain[...]
     net.drain()
 
 
-def run_layer(tok, cot, cs, bias, wqkv, wo, wgu, wdt):
+def run_layer(tok, cot, cs, bias, gain, wqkv, wo, wgate, wup, wdt):
     tokens, width = tok.shape
     rows, packed = wqkv.shape
     qcols = wo.shape[1]
@@ -1076,11 +1155,14 @@
     out_shape = [
         jax.ShapeDtypeStruct((tokens, width), BF16),
         jax.ShapeDtypeStruct((tokens, width), BF16),
-        jax.ShapeDtypeStruct((8, width), F32),
-        jax.ShapeDtypeStruct((rows, packed), F32),
+        jax.ShapeDtypeStruct((8, rows), F32),
         jax.ShapeDtypeStruct((rows, qcols), F32),
-        jax.ShapeDtypeStruct((2, rows, 2 * ff), F32),
-        jax.ShapeDtypeStruct((drows, ff), F32),
+        jax.ShapeDtypeStruct((rows, kw // 2), F32),
+        jax.ShapeDtypeStruct((rows, kw // 2), F32),
+        jax.ShapeDtypeStruct((rows, qcols), F32),
+        jax.ShapeDtypeStruct((rows, 2 * ff), F32),
+        jax.ShapeDtypeStruct((rows, 2 * ff), F32),
+        jax.ShapeDtypeStruct((ff, drows), F32),
     ]
 
     def vm(*shape, dtype=BF16):
@@ -1090,6 +1172,8 @@
         vm(2 * tokens, 256, dtype=F32),
         vm(2, 8, keys, dtype=F32),
         vm(tokens, width),
+        vm(n_ctx, 8, rows, dtype=F32),
+        vm(8, width, dtype=F32),
         vm(3, rows, packed),
         vm(3, rows, qcols),
         vm(2, width, packed),
@@ -1122,26 +1206,28 @@
         vm(3, tokens, width),
         vm(3, tokens, width),
         vm(2, width, ff),
-        vm(3, 2, 2 * rows, ff),
-        vm(2, 2 * rows, ff),
-        vm(2, 2, rows, ff),
+        vm(2, width, ff),
+        vm(2, 2, 2, rows, ff),
         vm(width, ff),
-        vm(3, width, ff),
-        vm(width, ff),
-        vm(drows, ff),
+        vm(2 * drows, ff),
+        vm(2 * drows, ff),
+        vm(2, drows, ff),
         vm(4, 4, rows, ff),
-        vm(4, 4, rows, 512),
+        vm(4, 4, rows, ff),
+        vm(4, 4, rows, 256),
         vm(3, rows, qcols),
-        vm(3, rows, packed),
         vm(3, rows, qcols),
-        vm(3, rows, packed),
+        vm(3, rows, kw),
+        vm(3, rows, qcols),
+        vm(3, rows, qcols),
+        vm(3, rows, kw),
+        vm(rows, kw, dtype=F32),
         vm(n_ctx, 2, 2 * kw, tokens),
         vm(4, 2, 2 * kw, tokens),
         vm(3, 2, 2 * kw, tokens),
         vm(3, 2, 2 * kw, tokens),
-        vm(8, 8, width, dtype=F32),
-        vm(2, 8, width, dtype=F32),
-        vm(3, 8, width, dtype=F32),
+        vm(3, 8, rows, dtype=F32),
+        vm(8, rows, dtype=F32),
         vm(2, 2 * tokens, packed),
         pltpu.SemaphoreType.DMA((N_SEM,)),
         pltpu.SemaphoreType.DMA((N_SEM,)),
@@ -1150,14 +1236,14 @@
     return pl.pallas_call(
         layer_kernel,
         out_shape=out_shape,
-        in_specs=[inside] * 8,
+        in_specs=[inside] * 10,
         out_specs=[inside] * len(out_shape),
         scratch_shapes=scratch,
         compiler_params=pltpu.CompilerParams(
             collective_id=0, has_side_effects=True, vmem_limit_bytes=VMEM_LIMIT
         ),
         name="layer",
-    )(tok, cot, cs, bias, wqkv, wo, wgu, wdt)
+    )(tok, cot, cs, bias, gain, wqkv, wo, wgate, wup, wdt)
 
 
 VMEM_LIMIT = 63 * 1024 * 1024
@@ -1177,29 +1263,24 @@
     limit = (ctx * seq_rows // block + 1) * block
     bias = jnp.where(jnp.arange(keys, dtype=jnp.int32) < limit, 0.0, VERY_NEGATIVE).astype(F32)
     bias = jnp.broadcast_to(bias[None, :], (8, keys))
-    gain_one = attn_gain.astype(F32)[:, None]
-    gain_two = mlp_gain.astype(F32)[:, None]
-    wqkv = (jnp.concatenate([w_query, w_key, w_value], 1).astype(F32) * gain_one).astype(BF16)
-    wgu = jnp.stack([(w_gate.astype(F32) * gain_two).astype(BF16), (w_up.astype(F32) * gain_two).astype(BF16)])
-    output, input_grad, gains, g_qkv, g_o, g_gu, g_dt = run_layer(
-        tokens[0], cotangent[0], cs, bias, wqkv, w_out, wgu, w_down.T
-    )
-    rows, qcols = w_query.shape
-    kcols = w_key.shape[1]
-    part = lax.dynamic_slice(gains, (0, ctx * rows), (2, rows))
-    g_qkv = g_qkv * gain_one
+    rows = w_query.shape[0]
+    gain = jnp.concatenate([attn_gain[None], mlp_gain[None], jnp.ones((6, rows), BF16)], 0).astype(F32)
+    wqkv = jnp.concatenate([w_query, w_key, w_value], 1)
+    output, input_grad, gains, g_q, g_k, g_v, g_o, g_gate, g_up, g_d = run_layer(
+        tokens[0], cotangent[0], cs, bias, gain, wqkv, w_out, w_gate, w_up, w_down.T
+    )
     return (
         output[None],
         input_grad[None],
-        part[0] / gain_one[:, 0],
-        g_qkv[:, :qcols],
-        g_qkv[:, qcols : qcols + kcols],
-        g_qkv[:, qcols + kcols :],
+        gains[0],
+        g_q,
+        g_k,
+        g_v,
         g_o,
-        part[1] / gain_two[:, 0],
-        g_gu[0] * gain_two,
-        g_gu[1] * gain_two,
-        g_dt.T,
+        gains[1],
+        g_gate,
+        g_up,
+        g_d,
     )
 
 

time: 301 us -> 265 us (0.88)
  Pallas kernels: 285 us -> 248 us
  local copies, waits for them, and re-layouts: 7.81 us -> 12.5 us
    pallas_call x1, Pallas kernels: 285 us -> 248 us  [run_layer(): pl.pallas_call(layer_kernel, out_shape=out_shape, in_specs=[inside] * 10,...]
    unnamed x28 -> x35, local copies, waits for them, and re-layouts: 4.05 us -> 9.61 us
where the time goes in v2:
time: 265 us
  Pallas kernels  248 us (94%)
  local copies, waits for them, and re-layouts  12.5 us (5%)
    pallas_call x1, Pallas kernels, run_layer(): pl.pallas_call(layer_kernel, out_shape=out_shape, in_specs=[inside] * 10,...  248 us
    unnamed x35, local copies, waits for them, and re-layouts  9.61 us

profile of v2, /device:TPU:0, one launch (start us, length us, event | category | flops | bytes accessed | tf_op | source)
XLA Modules:
  0.0 265.0 jit_solution(11246152216820076579)
XLA Ops:
  1.3 0.0 copy-start.10
  1.3 0.0 copy-start.11
  1.3 0.0 copy-start.12
  1.3 0.0 copy-start.9
  1.4 0.0 copy-start.8
  1.4 0.6 copy-done.10
  2.0 0.1 pad.5.clone
  2.1 0.0 copy-done.11
  2.1 0.0 copy-done.12
  2.1 0.7 maximum_convert_fusion.gain
  2.8 0.6 broadcast_in_dim.33.bias
  3.4 0.0 copy-done.9
  3.4 0.0 copy-done.8
  3.4 1.7 pad_maximum_fusion.wqkv
  5.1 0.3 multiply_sine_fusion
  5.4 0.8 concatenate.9.cs
  6.2 248.5 %layer.1 = (bf16[128,1152]{1,0:T(8,128)(2,1)}, bf16[128,1152]{1,0:T(8,128)(2,1)}, f32[8,144]{1,0:T(8,128)}, f32[144,288]{1,0:T(8,128)}, f32[144,96]{1,0:T(8,128)...) custom-call(bf16[128,1152]{1,0:T(8,128)(2,1)} %bitcast.14, ...), custom_call_target="tpu_custom_call" | custom-call | tf_op jit(solution)/shard_map/layer/pallas_call | solution.py:1236
  254.7 1.3 fusion.2
  256.0 2.1 copy.26
  258.1 0.7 copy.36
  258.8 0.4 copy-done.2
  259.2 0.7 copy.37
  259.9 0.3 copy-done.5
  260.2 0.7 copy.38
  260.9 0.2 copy-done.7
  261.1 0.6 copy.39
  261.8 0.0 copy-done.6
  261.8 0.6 copy.40
  262.4 0.7 copy.41
  263.1 0.8 copy.42
  263.9 0.4 copy-done
  264.3 0.8 copy.43
  (17 shorter events, 0.0 us)
Async XLA Ops:
  1.3 0.7 copy-start.10
  1.3 0.7 copy-start.11
  1.3 0.7 copy-start.12
  1.3 2.1 copy-start.9
  1.4 2.0 copy-start.8
  256.0 2.1 copy-start.3
  258.1 1.1 copy-start.2
  259.2 1.0 copy-start.5
  260.2 0.9 copy-start.7
  260.2 1.5 copy-start.6
  260.2 2.2 copy-start.4
  261.1 2.0 copy-start.1
  263.1 1.2 copy-start

commit v3 on v2

--- a/solution.py
+++ b/solution.py
@@ -498,7 +498,7 @@
     o_out, o_ing, o_gain, o_q, o_k, o_v, o_o, o_gate, o_up, o_d,
     csf, b2, x2, gb, grow, wqz, woz, wq, wok, wg8, wd8, c8, n8, n1, qf, kvf, kv, q6, p6, o6, ab,
     mp, ml, mid, dmid, dmb, dm4, do6, act, pt, l1, s2, l2, l1o, s2o, l2o,
-    ggu, lgu, lf, gdt, lgd, sgd, ld, lo, lq, lk, so, sq, sk, lzo, lzq, lzk, kvg, dkv, lx, sx, lkz,
+    ggu, lgu, lf, gdt, lgd, sgd, ld, loy, lo, lqy, lqx, lky, lkx, so, sq, sk, lzo, lzq, lzk, kvg, dkv, lx, sx, lkz,
     lg, sg, dqk, send_sems, recv_sems,
 ):
     net = Wires(send_sems, recv_sems)
@@ -586,9 +586,24 @@
         inv = lax.rsqrt(jnp.mean(v * v, -1, keepdims=True) + EPSILON)
         return v * inv, inv
 
+    def gather_x(buf, slot):
+        net.send(buf.at[0], buf.at[4], slot + 2, dev(y, c, z, 1 - x))
+
+    def gather_z(buf, slot):
+        net.send(buf.at[0], buf.at[1], slot + 4, partner)
+        net.send(buf.at[0], buf.at[2], slot + 1, dev(y, c, zat(1), x))
+
+    def gather_pass(buf, slot, h):
+        net.recv(buf.at[2 * h], slot + h)
+        net.send(buf.at[2 * h], buf.at[2 * h + 1], slot + 4 + h, partner)
+        if h == 1:
+            net.send(buf.at[2], buf.at[6], slot + 3, dev(y, c, z, 1 - x))
+
+    r_c8 = net.slots(8)
     for k in range(1, 4):
         net.recv(wqz.at[k - 1], r_wqz + k)
         spread_qkv(k, wqz.at[k - 1])
+    gather_x(c8, r_c8)
 
     r_woz, r_wo = net.slots(4), net.slots(16)
 
@@ -654,6 +669,7 @@
         net.send(wo, woz.at[k - 1], r_woz + k, dev(y, c, zat(k), x))
     spread_wo(0, wo)
     send_ff(0)
+    gather_z(c8, r_c8)
 
     for k in range(4):
         for hx in range(2):
@@ -702,15 +718,6 @@
         net.recv(wq.at[0, at_x], slot)
         net.recv(wq.at[1, at_o], slot + 3)
 
-    def gather_start(buf, slot):
-        net.send(buf.at[0], buf.at[1], slot + 4, partner)
-        for h in range(1, 4):
-            net.send(buf.at[0], buf.at[2 * h], slot + h, dev(y, c, zat(h % 2), flip(x, h // 2)))
-
-    def gather_pass(buf, slot, h):
-        net.recv(buf.at[2 * h], slot + h)
-        net.send(buf.at[2 * h], buf.at[2 * h + 1], slot + 4 + h, partner)
-
     lane = lax.broadcasted_iota(jnp.int32, (2 * tokens, 128), 1)
     low_half = lax.rem(lane, HEAD_SIZE) < HEAD_SIZE // 2
 
@@ -737,10 +744,26 @@
     own_keys = pl.ds(off(ctx, tokens), tokens)
     for s in range(2):
         kv[s, own_keys] = kvf[s * tokens : (s + 1) * tokens].astype(BF16)
-    r_kz, r_kx = net.slots(4), net.slots(4)
-    for k in range(1, 4):
-        net.send(kv.at[:, own_keys], kv.at[:, own_keys], r_kz + k, dev(y, c, zat(k), x))
-    net.send(kv.at[:, own_keys], kv.at[:, own_keys], r_kx, dev(y, c, z, 1 - x))
+    r_kz, r_kx = net.slots(8), net.slots(8)
+
+    def kv_part(s, k, hx):
+        return kv.at[s, pl.ds(off(2 * zat(k) + flip(x, hx), tokens), tokens)]
+
+    for s in range(2):
+        part = kv_part(s, 0, 0)
+        for k in range(1, 4):
+            net.send(part, part, r_kz + 4 * s + k, dev(y, c, zat(k), x))
+        net.send(part, part, r_kx + 4 * s, dev(y, c, z, 1 - x))
+
+    def pass_kv(s, k):
+        part = kv_part(s, k, 0)
+        net.recv(part, r_kz + 4 * s + k)
+        net.send(part, part, r_kx + 4 * s + k, dev(y, c, z, 1 - x))
+
+    def take_kv(s):
+        for k in range(4):
+            net.recv(kv_part(s, k, 1), r_kx + 4 * s + k)
+
     send_ff(1)
     send_down()
 
@@ -752,43 +775,43 @@
                 s * tokens : (s + 1) * tokens, HEAD_SIZE * h : HEAD_SIZE * (h + 1)
             ].astype(BF16)
     for k in range(1, 4):
-        part = pl.ds(off(2 * zat(k) + x, tokens), tokens)
-        net.recv(kv.at[:, part], r_kz + k)
-        net.send(kv.at[:, part], kv.at[:, part], r_kx + k, dev(y, c, z, 1 - x))
-    r_c8 = net.slots(8)
-    gather_start(c8, r_c8)
+        pass_kv(0, k)
+    pass_kv(1, 1)
+    pass_kv(1, 2)
     for zz in range(2):
-        part = wok.at[2 * (1 - y), pl.ds(off(2 * zz + x, rows), rows)]
-        net.recv(part, r_wo + zz * 8 + 2)
-        net.send(part, part, r_wo + zz * 8 + 6, dev(y, c, z, 1 - x))
-        part = wok.at[2 * y + 1, pl.ds(off(2 * zz + 1 - x, rows), rows)]
-        net.recv(part, r_wo + zz * 8 + 5)
-        net.send(part, part, r_wo + zz * 8 + 7, dev(1 - y, c, z, x))
+        for cc in range(2):
+            part = wok.at[2 * y + cc, pl.ds(off(2 * zz + 1 - x, rows), rows)]
+            slot = r_wo + zz * 8 + 4 + cc
+            net.recv(part, slot)
+            net.send(part, part, slot + 2, dev(1 - y, c, z, x))
     pass_ff(0)
-    for k in range(4):
-        net.recv(kv.at[:, pl.ds(off(2 * zat(k) + 1 - x, tokens), tokens)], r_kx + k)
-
-    def attend(s, carry):
-        mask = b2[s][0:1, :]
-        for g in range(groups):
-            kg = kv[s, :, HEAD_SIZE * g : HEAD_SIZE * (g + 1)]
-            vg = kv[s, :, kw + HEAD_SIZE * g : kw + HEAD_SIZE * (g + 1)]
-            scores = dot_nt(q6[s * groups + g], kg) + mask
-            weights = jnp.exp(scores - jnp.max(scores, -1, keepdims=True))
-            probs = (weights * (1.0 / jnp.sum(weights, -1, keepdims=True))).astype(BF16)
-            p6[s * groups + g] = probs
-            got = dot_nn(probs, vg).astype(BF16)
-            o6[s * groups + g] = got
-            for i in range(per):
-                h = g * per + i
-                ab[pl.ds(off(s, tokens), tokens), HEAD_SIZE * h : HEAD_SIZE * (h + 1)] = got[
-                    i * tokens : (i + 1) * tokens
-                ]
-        return carry
-
-    lax.fori_loop(0, 2, attend, 0)
-
-    for hx, hy, cc in ((0, 0, 0), (0, 0, 1), (0, 1, 1), (1, 0, 0), (1, 1, 0), (1, 1, 1)):
+    take_kv(0)
+
+    def attend(s, g):
+        kg = kv[s, :, HEAD_SIZE * g : HEAD_SIZE * (g + 1)]
+        vg = kv[s, :, kw + HEAD_SIZE * g : kw + HEAD_SIZE * (g + 1)]
+        scores = dot_nt(q6[s * groups + g], kg) + b2[s, 0:1, :]
+        weights = jnp.exp(scores - jnp.max(scores, -1, keepdims=True))
+        probs = (weights * (1.0 / jnp.sum(weights, -1, keepdims=True))).astype(BF16)
+        p6[s * groups + g] = probs
+        got = dot_nn(probs, vg).astype(BF16)
+        o6[s * groups + g] = got
+        for i in range(per):
+            h = g * per + i
+            ab[s * tokens : (s + 1) * tokens, HEAD_SIZE * h : HEAD_SIZE * (h + 1)] = got[
+                i * tokens : (i + 1) * tokens
+            ]
+
+    attend(0, 0)
+    pass_kv(1, 3)
+    attend(0, 1)
+    gather_pass(c8, r_c8, 1)
+    attend(0, 2)
+    take_kv(1)
+    for g in range(groups):
+        attend(1, g)
+
+    for hx, hy, cc in ((0, 0, 0), (0, 0, 1), (0, 1, 0), (0, 1, 1), (1, 1, 0), (1, 1, 1)):
         for zz in range(2):
             net.recv(
                 wok.at[2 * flip(y, hy) + cc, pl.ds(off(2 * zz + flip(x, hx), rows), rows)],
@@ -805,13 +828,14 @@
         part = wd8.at[pl.ds(off(2 * y + cc, drows), drows)]
         net.recv(part, r_wd + cc)
         net.send(part, part, r_wy + cc, dev(1 - y, c, z, x))
-    for h in range(1, 4):
-        gather_pass(c8, r_c8, h)
+    gather_pass(c8, r_c8, 2)
+    gather_pass(c8, r_c8, 3)
     net.recv(ml, r_ml)
     mid[...] = tok[...].astype(F32) + mp[0] + ml[...]
     n8[0] = (normed(mid[...])[0] * grow[1:2]).astype(BF16)
     r_n8 = net.slots(8)
-    gather_start(n8, r_n8)
+    gather_z(n8, r_n8)
+    gather_x(n8, r_n8)
 
     net.recv(c8.at[1], r_c8 + 4)
     for h in range(1, 4):
@@ -948,45 +972,67 @@
     attn_all = ab[:, 0:qw]
     for part in range(4):
         act[qw * part : qw * (part + 1), 0:qcols] = dot_tn(attn_all, dm4[part]).astype(BF16)
-    r_go = net.slots(16)
-    for zz in range(2):
-        for hx in range(2):
-            for hy in range(2):
-                for hc in range(2):
-                    zt = 2 * c + zz
-                    to_dp = 2 * flip(y, hy) + flip(c, hc)
-                    at = pl.multiple_of(to_dp * qw + (2 * zz + flip(x, hx)) * rows, rows)
+    r_gy, r_go = net.slots(2), net.slots(8)
+    for cc in range(2):
+        net.send(
+            act.at[pl.ds(off(2 * (1 - y) + cc, qw), qw)], loy.at[cc], r_gy + cc, dev(1 - y, c, z, x)
+        )
+
+    def pass_go():
+        for cc in range(2):
+            net.recv(loy.at[cc], r_gy + cc)
+            at = pl.ds(off(2 * y + cc, qw), qw)
+            act[at] = (act[at].astype(F32) + loy[cc].astype(F32)).astype(BF16)
+        for hx in (1, 0):
+            for hc in range(2):
+                for zz in range(2):
+                    at = pl.multiple_of((2 * y + flip(c, hc)) * qw + (2 * zz + flip(x, hx)) * rows, rows)
                     src = act.at[pl.ds(at, rows)]
-                    dst = lo.at[zt, hx * 2 + hy]
-                    slot = r_go + zt * 4 + hx * 2 + hy
-                    if hx + hy + hc == 0:
+                    dst = lo.at[2 * c + zz, hx]
+                    slot = r_go + (2 * c + zz) * 2 + hx
+                    if hx + hc == 0:
                         net.keep(src, dst, slot)
                     else:
-                        net.send(src, dst, slot, dev(flip(y, hy), flip(c, hc), z, flip(x, hx)))
-
-    def attend_back(s):
-        for g in range(groups):
-            at = s * groups + g
-            kg = kv[s, :, HEAD_SIZE * g : HEAD_SIZE * (g + 1)]
-            vg = kv[s, :, kw + HEAD_SIZE * g : kw + HEAD_SIZE * (g + 1)]
-            dout = do6[at]
-            delta = jnp.sum(dout.astype(F32) * o6[at].astype(F32), -1, keepdims=True)
-            dprob = dot_nt(dout, vg)
-            dscore = (p6[at].astype(F32) * (dprob - delta)).astype(BF16)
-            dquery = dot_nn(dscore, kg) * scale
-            dkeys = dot_tn(q6[at], dscore)
-            dvals = dot_tn(dout, p6[at])
-            for t in range(n_ctx):
-                cols = slice(t * tokens, (t + 1) * tokens)
-                dkv[t, s, HEAD_SIZE * g : HEAD_SIZE * (g + 1)] = dkeys[:, cols].astype(BF16)
-                dkv[t, s, kw + HEAD_SIZE * g : kw + HEAD_SIZE * (g + 1)] = dvals[:, cols].astype(BF16)
-            for i in range(per):
-                h = g * per + i
-                qf[s * tokens : (s + 1) * tokens, HEAD_SIZE * h : HEAD_SIZE * (h + 1)] = dquery[
-                    i * tokens : (i + 1) * tokens
-                ]
-
-    attend_back(0)
+                        net.send(src, dst, slot, dev(y, flip(c, hc), z, flip(x, hx)))
+
+    def attend_back(s, g):
+        at = s * groups + g
+        kg = kv[s, :, HEAD_SIZE * g : HEAD_SIZE * (g + 1)]
+        vg = kv[s, :, kw + HEAD_SIZE * g : kw + HEAD_SIZE * (g + 1)]
+        dout = do6[at]
+        delta = jnp.sum(dout.astype(F32) * o6[at].astype(F32), -1, keepdims=True)
+        dprob = dot_nt(dout, vg)
+        dscore = (p6[at].astype(F32) * (dprob - delta)).astype(BF16)
+        dquery = dot_nn(dscore, kg) * scale
+        dkeys = dot_tn(q6[at], dscore)
+        dvals = dot_tn(dout, p6[at])
+        for t in range(n_ctx):
+            cols = slice(t * tokens, (t + 1) * tokens)
+            dkv[t, s, HEAD_SIZE * g : HEAD_SIZE * (g + 1)] = dkeys[:, cols].astype(BF16)
+            dkv[t, s, kw + HEAD_SIZE * g : kw + HEAD_SIZE * (g + 1)] = dvals[:, cols].astype(BF16)
+        for i in range(per):
+            h = g * per + i
+            qf[s * tokens : (s + 1) * tokens, HEAD_SIZE * h : HEAD_SIZE * (h + 1)] = dquery[
+                i * tokens : (i + 1) * tokens
+            ]
+
+    r_dx, r_dz = net.slots(8), net.slots(8)
+
+    def send_dkv(s):
+        for k in (1, 2, 3, 0):
+            net.send(
+                dkv.at[2 * zat(k) + 1 - x, s], lx.at[k, s], r_dx + 4 * s + k, dev(y, c, z, 1 - x)
+            )
+
+    def pass_dkv(s):
+        for k in range(1, 4):
+            net.recv(lx.at[k, s], r_dx + 4 * s + k)
+            sx[k - 1, s] = (dkv[2 * zat(k) + x, s].astype(F32) + lx[k, s].astype(F32)).astype(BF16)
+            net.send(sx.at[k - 1, s], lkz.at[k - 1, s], r_dz + 4 * s + k, dev(y, c, zat(k), x))
+
+    for g in range(groups):
+        attend_back(0, g)
+    send_dkv(0)
     r_gf = net.slots(4)
     for k in (3, 2, 1, 0):
         at = pl.ds(off(zat(k), 2 * rows), 2 * rows)
@@ -1008,40 +1054,86 @@
                 def _():
                     net.keep(src, dst, slot)
 
-    attend_back(1)
-    r_dx, r_dz = net.slots(4), net.slots(4)
-    for k in (1, 2, 3, 0):
-        net.send(dkv.at[2 * zat(k) + 1 - x], lx.at[k], r_dx + k, dev(y, c, z, 1 - x))
+    attend_back(1, 0)
+    pass_go()
+    attend_back(1, 1)
+    pass_dkv(0)
+    attend_back(1, 2)
+    send_dkv(1)
     for t in range(qf.shape[1] // 128):
         qf[:, 128 * t : 128 * (t + 1)] = turn(qf[:, 128 * t : 128 * (t + 1)], False)
+    grad = dot_tn(n1[...], qf[:, 0:qw].astype(BF16)).astype(BF16)
+    for t in range(n_ctx):
+        p6[t // 2, (t % 2) * rows : (t % 2 + 1) * rows, 0:qw] = grad[rows * t : rows * (t + 1)]
     for part in range(2):
         dqk[part, :, 0:qcols] = qf[:, qcols * part : qcols * (part + 1)].astype(BF16)
-        got = dot_tn(n1[...], dqk[part, :, 0:qcols]).astype(BF16)
-        for t in range(n_ctx):
-            p6[t // 2, (t % 2) * rows : (t % 2 + 1) * rows, ff * part : ff * part + qcols] = got[
-                rows * t : rows * (t + 1)
-            ]
+    r_qy, r_qx, r_zq = net.slots(4), net.slots(4), net.slots(4)
+    mine = c == y
 
     def send_grads(source, land, slot):
-        for k in (3, 2, 1, 0):
-            for hx in range(2):
-                for ct in range(2):
+        for k in range(4):
+            net.send(
+                source(zat(k), slice(0, 2)), land.at[zat(k)], slot + k, dev(1 - y, c, z, x),
+                only=jnp.logical_not(mine),
+            )
+
+    def add_y(source, land, slot, land_x, slot_x):
+        for k in range(4):
+
+            @pl.when(mine)
+            def _():
+                net.recv(land.at[zat(k)], slot + k)
+                here = source(zat(k), slice(0, 2))
+                here[...] = (here[...].astype(F32) + land[zat(k)].astype(F32)).astype(BF16)
+
+            net.send(
+                source(zat(k), 1 - x), land_x.at[k], slot_x + k, dev(y, c, z, 1 - x), only=mine
+            )
+
+    def add_x(source, land_x, slot_x, staged, arrived, slot_z):
+        wide_part = arrived.shape[2]
+        for k in (1, 2, 3, 0):
+
+            @pl.when(mine)
+            def _():
+                net.recv(land_x.at[k], slot_x + k)
+                staged[k] = (source(zat(k), x)[...].astype(F32) + land_x[k].astype(F32)).astype(BF16)
+
+            for cc in range(2):
+                first = cc * (staged.shape[2] - wide_part)
+                src = staged.at[k, :, pl.ds(first, wide_part)]
+                if k:
+                    net.send(src, arrived.at[k], slot_z + k, dev(y, cc, zat(k), x), only=mine)
+                else:
+
+                    @pl.when(jnp.logical_and(mine, c == cc))
+                    def _():
+                        net.keep(src, arrived.at[k], slot_z)
+
                     net.send(
-                        source(zat(k), flip(x, hx), ct),
-                        land.at[k, hx * 2 + y_c],
-                        slot + k * 4 + hx * 2 + y_c,
-                        dev(c, ct, z, flip(x, hx)),
-                        is_self=jnp.logical_and(y == c, c == ct) if hx == 0 else None,
+                        src, arrived.at[k], slot_z, dev(y, cc, z, x),
+                        only=jnp.logical_and(mine, c != cc),
                     )
 
-    for k in range(1, 4):
-        net.recv(lx.at[k], r_dx + k)
-        sx[k - 1] = (dkv[2 * zat(k) + x].astype(F32) + lx[k].astype(F32)).astype(BF16)
-        net.send(sx.at[k - 1], lkz.at[k - 1], r_dz + k, dev(y, c, zat(k), x))
-    r_gq = net.slots(16)
-    send_grads(
-        lambda zt, xt, ct: p6.at[zt, pl.ds(off(xt, rows), rows), pl.ds(ff * ct, ff)], lq, r_gq
-    )
+    def add_z(out, arrived, slot_z, staged):
+        total = 0.0
+        for k in (1, 2, 3, 0):
+            net.recv(arrived.at[k], slot_z + k)
+            total = total + arrived[k].astype(F32)
+        count = out.shape[1]
+        skip = count - (staged.shape[2] - arrived.shape[2])
+        out[...] = jnp.where(c == 0, total[:, 0:count], total[:, skip : skip + count])
+
+    def in_p6(zt, xt):
+        at = pl.ds(0, 2 * rows) if isinstance(xt, slice) else pl.ds(off(xt, rows), rows)
+        return p6.at[zt, at, pl.ds(0, qf.shape[1])]
+
+    def in_wg8(zt, xt):
+        at = pl.ds(off(zt, 2 * rows), 2 * rows) if isinstance(xt, slice) else pl.ds(off(2 * zt + xt, rows), rows)
+        return wg8.at[0, at]
+
+    send_grads(in_p6, lqy, r_qy)
+    pass_dkv(1)
     for h in range(1, 4):
         reduce_pass(pt, l1o, s2o, l2o, r_out, h)
     mid[...] = mid[...] + reduce_own(pt, l1o, r_out)
@@ -1050,8 +1142,8 @@
         for k in (1, 2, 3, 0):
             at = zat(k) if absolute else k
             part = 0.0
-            for h in range(4):
-                net.recv(land.at[at, h], slot + at * 4 + h)
+            for h in range(2):
+                net.recv(land.at[at, h], slot + at * 2 + h)
                 part = part + land[at, h, :, 0 : out.shape[1]].astype(F32)
             if k == 0:
                 out[...] = part
@@ -1064,16 +1156,17 @@
             net.recv(arrived.at[k - 1], slot + k)
             out[...] = out[...] + arrived[k - 1].astype(F32)
 
-    r_zo, r_zq, r_zk = net.slots(4), net.slots(4), net.slots(4)
+    r_zo = net.slots(4)
     attn_pass(lo, o_o, so, lzo, r_zo, r_go, True)
-
-    net.recv(lx.at[0], r_dx)
-    total = dkv[2 * z + x].astype(F32) + lx[0].astype(F32)
-    for k in range(1, 4):
-        net.recv(lkz.at[k - 1], r_dz + k)
-        total = total + lkz[k - 1].astype(F32)
+    add_y(in_p6, lqy, r_qy, lqx, r_qx)
+
     for s in range(2):
-        kvf[s * tokens : (s + 1) * tokens] = total[s].T
+        net.recv(lx.at[0, s], r_dx + 4 * s)
+        total = dkv[2 * z + x, s].astype(F32) + lx[0, s].astype(F32)
+        for k in range(1, 4):
+            net.recv(lkz.at[k - 1, s], r_dz + 4 * s + k)
+            total = total + lkz[k - 1, s].astype(F32)
+        kvf[s * tokens : (s + 1) * tokens] = total.T
     turn_keys(False)
     for part in range(2):
         dqk[part, :, qcols : qcols + kcols] = kvf[:, kcols * part : kcols * (part + 1)].astype(BF16)
@@ -1081,18 +1174,19 @@
     for finish in ff_passed:
         net.done(finish)
     for part in range(2):
-        wg8[part, :, 0 : 2 * kcols] = dot_tn(n1[...], dqk[part, :, qcols:]).astype(BF16)
-    r_gk = net.slots(16)
-    send_grads(
-        lambda zt, xt, ct: wg8.at[ct, pl.ds(off(2 * zt + xt, rows), rows), pl.ds(0, 256)], lk, r_gk
-    )
+        wg8[0, :, 2 * kcols * part : 2 * kcols * (part + 1)] = dot_tn(
+            n1[...], dqk[part, :, qcols:]
+        ).astype(BF16)
+    r_ky, r_kx2, r_zk = net.slots(4), net.slots(4), net.slots(4)
+    send_grads(in_wg8, lky, r_ky)
     net.done(mp_sent)
     got = dot_nt(dqk[0], wq[0]) + dot_nt(dqk[1], wq[1])
     for s in range(2):
         mp[s] = got[s * tokens : (s + 1) * tokens]
     r_dn1 = net.slots(1)
     net.send(mp.at[1], ml, r_dn1, partner)
-    attn_pass(lq, o_q, sq, lzq, r_zq, r_gq, False)
+    add_x(in_p6, lqx, r_qx, sq, lzq, r_zq)
+    add_y(in_wg8, lky, r_ky, lkx, r_kx2)
     net.recv(ml, r_dn1)
     total = mp[0] + ml[...]
     normed_one, inv_one = normed(tok[...])
@@ -1101,7 +1195,7 @@
         dmid[...]
         + inv_one * (total - normed_one * jnp.mean(total * normed_one, -1, keepdims=True))
     ).astype(BF16)
-    attn_pass(lk, kvg, sk, lzk, r_zk, r_gk, False)
+    add_x(in_wg8, lkx, r_kx2, sk, lzk, r_zk)
 
     o_out[...] = (mid[...] + reduce_end(l2o, r_out)).astype(BF16)
     gains = [0.0, 0.0]
@@ -1119,9 +1213,9 @@
         net.recv(ld.at[zh], r_ld + zh)
     o_d[...] = (ld[0].astype(F32) + ld[1].astype(F32)).T
     attn_end(o_o, lzo, r_zo)
-    attn_end(o_q, lzq, r_zq)
+    add_z(o_q, lzq, r_zq, sq)
     gains[0] = jnp.sum(o_q[...] * wqkv[:, 0:qcols].astype(F32), 1, keepdims=True)
-    attn_end(kvg, lzk, r_zk)
+    add_z(kvg, lzk, r_zk, sk)
     gains[0] = gains[0] + jnp.sum(kvg[...] * wqkv[:, qcols:].astype(F32), 1, keepdims=True)
     o_k[...] = kvg[:, 0:kcols]
     o_v[...] = kvg[:, kcols:]
@@ -1212,15 +1306,18 @@
         vm(2 * drows, ff),
         vm(2 * drows, ff),
         vm(2, drows, ff),
-        vm(4, 4, rows, ff),
-        vm(4, 4, rows, ff),
-        vm(4, 4, rows, 256),
+        vm(2, qw, ff),
+        vm(4, 2, rows, ff),
+        vm(4, 2 * rows, wide),
+        vm(4, rows, wide),
+        vm(4, 2 * rows, ff),
+        vm(4, rows, ff),
         vm(3, rows, qcols),
+        vm(4, rows, wide),
+        vm(4, rows, ff),
         vm(3, rows, qcols),
-        vm(3, rows, kw),
-        vm(3, rows, qcols),
-        vm(3, rows, qcols),
-        vm(3, rows, kw),
+        vm(4, rows, ff),
+        vm(4, rows, 256),
         vm(rows, kw, dtype=F32),
         vm(n_ctx, 2, 2 * kw, tokens),
         vm(4, 2, 2 * kw, tokens),

time: 265 us -> 249 us (0.940)
  Pallas kernels: 248 us -> 231 us
    pallas_call x1, Pallas kernels: 248 us -> 231 us  [run_layer(): pl.pallas_call(layer_kernel, out_shape=out_shape, in_specs=[inside] * 10,...]
where the time goes in v3:
time: 249 us; the launch traced here: 248 us
  Pallas kernels  231 us (93%)
  local copies, waits for them, and re-layouts  12.5 us (5%)
  other arithmetic  2.64 us (1%)
    pallas_call x1, Pallas kernels, run_layer(): pl.pallas_call(layer_kernel, out_shape=out_shape, in_specs=[inside] * 10,...  231 us
    unnamed x35, local copies, waits for them, and re-layouts  9.61 us

profile of v3, /device:TPU:0, one launch (start us, length us, event | category | flops | bytes accessed | tf_op | source)
XLA Modules:
  0.0 248.1 jit_solution(16866746286644525585)
XLA Ops:
  1.3 0.0 copy-start.10
  1.3 0.0 copy-start.11
  1.3 0.0 copy-start.12
  1.3 0.0 copy-start.9
  1.4 0.0 copy-start.8
  1.4 0.6 copy-done.10
  2.0 0.1 pad.5.clone
  2.1 0.0 copy-done.11
  2.1 0.0 copy-done.12
  2.1 0.7 maximum_convert_fusion.gain
  2.8 0.6 broadcast_in_dim.33.bias
  3.4 0.0 copy-done.9
  3.4 0.0 copy-done.8
  3.4 1.7 pad_maximum_fusion.wqkv
  5.1 0.3 multiply_sine_fusion
  5.4 0.8 concatenate.9.cs
  6.2 231.5 %layer.1 = (bf16[128,1152]{1,0:T(8,128)(2,1)}, bf16[128,1152]{1,0:T(8,128)(2,1)}, f32[8,144]{1,0:T(8,128)}, f32[144,288]{1,0:T(8,128)}, f32[144,96]{1,0:T(8,128)...) custom-call(bf16[128,1152]{1,0:T(8,128)(2,1)} %bitcast.14, ...), custom_call_target="tpu_custom_call" | custom-call | tf_op jit(solution)/shard_map/layer/pallas_call | solution.py:1333
  237.7 1.3 fusion.2
  239.0 2.1 copy.26
  241.1 0.7 copy.36
  241.8 0.4 copy-done.2
  242.2 0.7 copy.37
  242.9 0.3 copy-done.5
  243.3 0.7 copy.38
  243.9 0.2 copy-done.7
  244.2 0.6 copy.39
  244.8 0.0 copy-done.6
  244.8 0.6 copy.40
  245.4 0.7 copy.41
  246.1 0.8 copy.42
  246.9 0.4 copy-done
  247.3 0.8 copy.43
  (17 shorter events, 0.0 us)
Async XLA Ops:
  1.3 0.7 copy-start.10
  1.3 0.7 copy-start.11
  1.3 0.7 copy-start.12
  1.3 2.1 copy-start.9
  1.4 2.0 copy-start.8
  239.0 2.1 copy-start.3
  241.1 1.1 copy-start.2
  242.2 1.0 copy-start.5
  243.2 0.9 copy-start.7
  243.2 1.5 copy-start.6
  243.2 2.2 copy-start.4
  244.2 2.0 copy-start.1
  246.1 1.2 copy-start

commit v4 on v3

--- a/solution.py
+++ b/solution.py
@@ -1,5 +1,6 @@
 import jax
 import jax.numpy as jnp
+import numpy as np
 from jax import lax
 from jax.experimental import pallas as pl
 from jax.experimental.pallas import tpu as pltpu
@@ -490,13 +491,14 @@
         self.pending = []
 
 
-N_SEM = 256
+N_SEM = 288
+FREQUENCY = np.float32(THETA) ** (-(np.arange(HEAD_SIZE // 2, dtype=np.float32) * 2.0 / HEAD_SIZE)).astype(np.float32)
 
 
 def layer_kernel(
-    tok, cot, cs, bias, gain, wqkv, wo, wgate, wup, wdt,
-    o_out, o_ing, o_gain, o_q, o_k, o_v, o_o, o_gate, o_up, o_d,
-    csf, b2, x2, gb, grow, wqz, woz, wq, wok, wg8, wd8, c8, n8, n1, qf, kvf, kv, q6, p6, o6, ab,
+    tok, cot, pos, blk, gain_one, gain_two, wquery, wkey, wvalue, wo, wgate, wup, wdt,
+    o_out, o_ing, o_gain_one, o_gain_two, o_q, o_k, o_v, o_o, o_gate, o_up, o_d,
+    wqkv, gain, csf, b2, x2, gb, grow, wqz, woz, wq, wok, wg8, wd8, c8, n8, n1, qf, kvf, kv, q6, p6, o6, ab,
     mp, ml, mid, dmid, dmb, dm4, do6, act, pt, l1, s2, l2, l1o, s2o, l2o,
     ggu, lgu, lf, gdt, lgd, sgd, ld, loy, lo, lqy, lqx, lky, lkx, so, sq, sk, lzo, lzq, lzk, kvg, dkv, lx, sx, lkz,
     lg, sg, dqk, send_sems, recv_sems,
@@ -509,9 +511,9 @@
     z_hi, z_lo = z // 2, lax.rem(z, 2)
     y_c = y + c - 2 * y * c
     tokens, width = tok.shape
-    rows = wqkv.shape[0]
+    rows = wquery.shape[0]
     qcols = wo.shape[1]
-    kcols = (wqkv.shape[1] - qcols) // 2
+    kcols = wkey.shape[1]
     ff = wdt.shape[1]
     drows = wdt.shape[0]
     qw = 2 * qcols
@@ -536,6 +538,15 @@
         return pl.multiple_of(value * step, step)
 
     partner = dev(y, 1 - c, z, x)
+    middle = z_hi != z_lo
+
+    wqkv[:, 0:qcols] = wquery[...]
+    wqkv[:, qcols : qcols + kcols] = wkey[...]
+    wqkv[:, qcols + kcols :] = wvalue[...]
+    row = lax.broadcasted_iota(jnp.int32, gain.shape, 0)
+    gain[...] = jnp.where(
+        row == 0, gain_one[...].astype(F32).reshape(1, rows), jnp.where(row == 1, gain_two[...].astype(F32).reshape(1, rows), 1.0)
+    )
 
     barrier = pltpu.get_barrier_semaphore()
     for k in range(4):
@@ -552,8 +563,6 @@
 
     r_tok = net.slots(3)
     net.send(tok, x2, r_tok, partner)
-    net.send(cs, csf.at[pl.ds(tokens, tokens)], r_tok + 1, partner)
-    net.send(bias, b2.at[1], r_tok + 2, partner)
     r_g = net.slots(8)
     r_wqz, r_wq = net.slots(4), net.slots(16)
 
@@ -568,16 +577,36 @@
                 is_self=(c == y) if hx + hy == 0 else None,
             )
 
-    for k in range(1, 4):
-        net.send(wqkv, wqz.at[k - 1], r_wqz + k, dev(y, c, zat(k), x))
+    def z_start(src, land, slot):
+        for k in range(1, 4):
+            net.send(src, land(k), slot + k, dev(y, c, zat(k), x), only=middle if k == 3 else None)
+
+    def z_relay(here, there, slot):
+        net.send(here, there, slot + 3, dev(y, c, zat(1), x), only=middle)
+
+    z_start(wqkv, lambda k: wqz.at[k - 1], r_wqz)
     spread_qkv(0, wqkv)
     for k in range(4):
         for hx in range(2):
             if k + hx:
                 net.send(gain, gb.at[ctx], r_g + 2 * k + hx, dev(y, c, zat(k), flip(x, hx)))
 
-    csf[0:tokens] = cs[...]
-    b2[0] = bias[...]
+    across = lax.broadcasted_iota(jnp.int32, (tokens, 128), 1)
+    entry = lax.rem(across, HEAD_SIZE // 2)
+    frequency = jnp.zeros((tokens, 128), F32)
+    for i in range(HEAD_SIZE // 2):
+        frequency = jnp.where(entry == i, float(FREQUENCY[i]), frequency)
+    places = jnp.broadcast_to(pos[...].astype(F32), (tokens, tokens)).T
+    angles = places * frequency
+    sine = jnp.sin(angles)
+    csf[0:tokens, 0:128] = jnp.cos(angles)
+    csf[0:tokens, 128:256] = jnp.where(lax.rem(across, HEAD_SIZE) < HEAD_SIZE // 2, -sine, sine)
+    inverse = 1.0 / blk[0].astype(F32)
+    key = lax.broadcasted_iota(jnp.int32, (8, keys), 1).astype(F32)
+    own_block = jnp.floor(jnp.full((8, keys), ctx * tokens, jnp.int32).astype(F32) * inverse)
+    b2[0] = jnp.where(jnp.floor(key * inverse) <= own_block, 0.0, VERY_NEGATIVE)
+    net.send(csf.at[pl.ds(0, tokens)], csf.at[pl.ds(tokens, tokens)], r_tok + 1, partner)
+    net.send(b2.at[0], b2.at[1], r_tok + 2, partner)
     gb[ctx] = gain[...]
     c8[0] = cot[...]
 
@@ -600,8 +629,10 @@
             net.send(buf.at[2], buf.at[6], slot + 3, dev(y, c, z, 1 - x))
 
     r_c8 = net.slots(8)
-    for k in range(1, 4):
+    for k in (1, 2, 3):
         net.recv(wqz.at[k - 1], r_wqz + k)
+        if k == 2:
+            z_relay(wqz.at[1], wqz.at[2], r_wqz)
         spread_qkv(k, wqz.at[k - 1])
     gather_x(c8, r_c8)
 
@@ -637,15 +668,15 @@
 
     def pass_ff(m):
         for i in range(n_ctx):
-            part = wg8.at[m, pl.ds(rows * i, rows)]
+            at = 2 * zat(i // 2) + flip(x, i % 2)
+            part = wg8.at[m, pl.ds(off(at, rows), rows)]
+            slot = r_gu + m * 8 + at
 
             @pl.when(home)
             def _():
-                net.recv(part, r_gu + m * 8 + i)
-
-            ff_passed.append(
-                net.send(part, part, r_gu + m * 8 + i, dev(1 - y, c, z, x), only=home)
-            )
+                net.recv(part, slot)
+
+            ff_passed.append(net.send(part, part, slot, dev(1 - y, c, z, x), only=home))
 
     def take_ff(m):
         for i in range(n_ctx):
@@ -665,8 +696,7 @@
                 is_self=jnp.logical_and(z == 2 * zh + z_x, c == z_lo),
             )
 
-    for k in range(1, 4):
-        net.send(wo, woz.at[k - 1], r_woz + k, dev(y, c, zat(k), x))
+    z_start(wo, lambda k: woz.at[k - 1], r_woz)
     spread_wo(0, wo)
     send_ff(0)
     gather_z(c8, r_c8)
@@ -701,6 +731,8 @@
         net.send(wq.at[1, at_x], wq.at[1, at_x], slot + 3, dev(y, c, z, 1 - x), only=(c != y))
     for k in range(1, 4):
         net.recv(woz.at[k - 1], r_woz + k)
+        if k == 2:
+            z_relay(woz.at[1], woz.at[2], r_woz)
         spread_wo(k, woz.at[k - 1])
     for k in range(4):
         at_x = pl.ds(off(2 * zat(k) + x, rows), rows)
@@ -751,13 +783,14 @@
 
     for s in range(2):
         part = kv_part(s, 0, 0)
-        for k in range(1, 4):
-            net.send(part, part, r_kz + 4 * s + k, dev(y, c, zat(k), x))
+        z_start(part, lambda k: part, r_kz + 4 * s)
         net.send(part, part, r_kx + 4 * s, dev(y, c, z, 1 - x))
 
     def pass_kv(s, k):
         part = kv_part(s, k, 0)
         net.recv(part, r_kz + 4 * s + k)
+        if k == 2:
+            z_relay(part, part, r_kz + 4 * s)
         net.send(part, part, r_kx + 4 * s + k, dev(y, c, z, 1 - x))
 
     def take_kv(s):
@@ -779,11 +812,12 @@
     pass_kv(1, 1)
     pass_kv(1, 2)
     for zz in range(2):
-        for cc in range(2):
-            part = wok.at[2 * y + cc, pl.ds(off(2 * zz + 1 - x, rows), rows)]
-            slot = r_wo + zz * 8 + 4 + cc
-            net.recv(part, slot)
-            net.send(part, part, slot + 2, dev(1 - y, c, z, x))
+        part = wok.at[2 * (1 - y), pl.ds(off(2 * zz + x, rows), rows)]
+        net.recv(part, r_wo + zz * 8 + 2)
+        net.send(part, part, r_wo + zz * 8 + 6, dev(y, c, z, 1 - x))
+        part = wok.at[2 * y + 1, pl.ds(off(2 * zz + 1 - x, rows), rows)]
+        net.recv(part, r_wo + zz * 8 + 5)
+        net.send(part, part, r_wo + zz * 8 + 7, dev(1 - y, c, z, x))
     pass_ff(0)
     take_kv(0)
 
@@ -811,7 +845,7 @@
     for g in range(groups):
         attend(1, g)
 
-    for hx, hy, cc in ((0, 0, 0), (0, 0, 1), (0, 1, 0), (0, 1, 1), (1, 1, 0), (1, 1, 1)):
+    for hx, hy, cc in ((0, 0, 0), (0, 0, 1), (0, 1, 1), (1, 0, 0), (1, 1, 0), (1, 1, 1)):
         for zz in range(2):
             net.recv(
                 wok.at[2 * flip(y, hy) + cc, pl.ds(off(2 * zz + flip(x, hx), rows), rows)],
@@ -1211,7 +1245,7 @@
             )
     for zh in range(2):
         net.recv(ld.at[zh], r_ld + zh)
-    o_d[...] = (ld[0].astype(F32) + ld[1].astype(F32)).T
+    o_d[...] = ld[0].astype(F32) + ld[1].astype(F32)
     attn_end(o_o, lzo, r_zo)
     add_z(o_q, lzq, r_zq, sq)
     gains[0] = jnp.sum(o_q[...] * wqkv[:, 0:qcols].astype(F32), 1, keepdims=True)
@@ -1229,17 +1263,27 @@
     for h in range(1, 4):
         net.recv(lg.at[h - 1], r_lg + h)
         total = total + lg[h - 1]
-    o_gain[...] = total / gain[...]
+    total = total / gain[...]
+    o_gain_one[...] = total[0:1]
+    o_gain_two[...] = total[1:2]
     net.drain()
 
 
-def run_layer(tok, cot, cs, bias, gain, wqkv, wo, wgate, wup, wdt):
+def hand_over(*refs):
+    count = len(refs) // 2
+    copies = [pltpu.make_async_copy(refs[i], refs[count + i], refs[-1].at[i]) for i in range(count)]
+    for copy in copies:
+        copy.start()
+    for copy in copies:
+        copy.wait()
+
+
+def run_layer(n_ctx, tok, cot, pos, blk, gain_one, gain_two, wquery, wkey, wvalue, wo, wgate, wup, wdt):
     tokens, width = tok.shape
-    rows, packed = wqkv.shape
-    qcols = wo.shape[1]
+    rows, qcols = wquery.shape
+    packed = qcols + 2 * wkey.shape[1]
     drows, ff = wdt.shape
-    keys = bias.shape[1]
-    n_ctx = keys // tokens
+    keys = n_ctx * tokens
     qw = 2 * qcols
     kw = packed - qcols
     groups = kw // HEAD_SIZE
@@ -1249,20 +1293,23 @@
     out_shape = [
         jax.ShapeDtypeStruct((tokens, width), BF16),
         jax.ShapeDtypeStruct((tokens, width), BF16),
-        jax.ShapeDtypeStruct((8, rows), F32),
+        jax.ShapeDtypeStruct((1, rows), F32),
+        jax.ShapeDtypeStruct((1, rows), F32),
         jax.ShapeDtypeStruct((rows, qcols), F32),
         jax.ShapeDtypeStruct((rows, kw // 2), F32),
         jax.ShapeDtypeStruct((rows, kw // 2), F32),
         jax.ShapeDtypeStruct((rows, qcols), F32),
         jax.ShapeDtypeStruct((rows, 2 * ff), F32),
         jax.ShapeDtypeStruct((rows, 2 * ff), F32),
-        jax.ShapeDtypeStruct((ff, drows), F32),
+        jax.ShapeDtypeStruct((drows, ff), F32),
     ]
 
     def vm(*shape, dtype=BF16):
         return pltpu.VMEM(shape, dtype)
 
     scratch = [
+        vm(rows, packed),
+        vm(8, rows, dtype=F32),
         vm(2 * tokens, 256, dtype=F32),
         vm(2, 8, keys, dtype=F32),
         vm(tokens, width),
@@ -1330,17 +1377,26 @@
         pltpu.SemaphoreType.DMA((N_SEM,)),
     ]
     inside = pl.BlockSpec(memory_space=pltpu.VMEM)
-    return pl.pallas_call(
+    outs = pl.pallas_call(
         layer_kernel,
         out_shape=out_shape,
-        in_specs=[inside] * 10,
+        in_specs=[inside] * 3 + [pl.BlockSpec(memory_space=pltpu.SMEM)] + [inside] * 9,
         out_specs=[inside] * len(out_shape),
         scratch_shapes=scratch,
         compiler_params=pltpu.CompilerParams(
             collective_id=0, has_side_effects=True, vmem_limit_bytes=VMEM_LIMIT
         ),
         name="layer",
-    )(tok, cot, cs, bias, gain, wqkv, wo, wgate, wup, wdt)
+    )(tok, cot, pos, blk, gain_one, gain_two, wquery, wkey, wvalue, wo, wgate, wup, wdt)
+    anywhere = pl.BlockSpec(memory_space=pl.ANY)
+    return pl.pallas_call(
+        hand_over,
+        out_shape=out_shape,
+        in_specs=[inside] * len(out_shape),
+        out_specs=[anywhere] * len(out_shape),
+        scratch_shapes=[pltpu.SemaphoreType.DMA((len(out_shape),))],
+        name="hand_over",
+    )(*outs)
 
 
 VMEM_LIMIT = 63 * 1024 * 1024
@@ -1350,34 +1406,22 @@
     tokens, positions, block_sizes, attn_gain, w_query, w_key, w_value, w_out, mlp_gain,
     w_gate, w_up, w_down, cotangent,
 ):
-    seq_rows, width = tokens.shape[1:]
-    ctx = lax.axis_index("ctx")
-    angles = angles_of(positions[0])
-    cosine, sine = jnp.cos(angles), jnp.sin(angles)
-    cs = jnp.concatenate([cosine] * 4 + [-sine, sine] * 2, 1)
-    keys = seq_rows * lax.axis_size("ctx")
-    block = block_sizes[0]
-    limit = (ctx * seq_rows // block + 1) * block
-    bias = jnp.where(jnp.arange(keys, dtype=jnp.int32) < limit, 0.0, VERY_NEGATIVE).astype(F32)
-    bias = jnp.broadcast_to(bias[None, :], (8, keys))
-    rows = w_query.shape[0]
-    gain = jnp.concatenate([attn_gain[None], mlp_gain[None], jnp.ones((6, rows), BF16)], 0).astype(F32)
-    wqkv = jnp.concatenate([w_query, w_key, w_value], 1)
-    output, input_grad, gains, g_q, g_k, g_v, g_o, g_gate, g_up, g_d = run_layer(
-        tokens[0], cotangent[0], cs, bias, gain, wqkv, w_out, w_gate, w_up, w_down.T
+    output, input_grad, g_one, g_two, g_q, g_k, g_v, g_o, g_gate, g_up, g_d = run_layer(
+        lax.axis_size("ctx"), tokens[0], cotangent[0], positions, block_sizes, attn_gain,
+        mlp_gain, w_query, w_key, w_value, w_out, w_gate, w_up, w_down.T,
     )
     return (
         output[None],
         input_grad[None],
-        gains[0],
+        g_one[0],
         g_q,
         g_k,
         g_v,
         g_o,
-        gains[1],
+        g_two[0],
         g_gate,
         g_up,
-        g_d,
+        g_d.T,
     )
 
 

time: 249 us -> 235 us (0.944)
  local copies, waits for them, and re-layouts: 12.5 us -> 0 us
  other arithmetic: 2.64 us -> 0 us
    unnamed x35 -> x0, local copies, waits for them, and re-layouts: 9.61 us -> none
    pallas_call x1 -> x2, Pallas kernels: 231 us -> 233 us  [the longest x1 230 us: run_layer(): pl.pallas_call(layer_kernel, out_shape=out_shape, in_specs=[inside] * 3 +...]
where the time goes in v4:
time: 235 us
  Pallas kernels  233 us (99%)
    pallas_call x1, Pallas kernels, run_layer(): pl.pallas_call(layer_kernel, out_shape=out_shape, in_specs=[inside] * 3 +...  230 us

profile of v4, /device:TPU:0, one launch (start us, length us, event | category | flops | bytes accessed | tf_op | source)
XLA Modules:
  0.0 234.7 jit_solution(9122290147122431274)
XLA Ops:
  1.3 230.0 %layer.1 = (bf16[128,1152]{1,0:T(8,128)(2,1)}, bf16[128,1152]{1,0:T(8,128)(2,1)}, f32[1,144]{1,0:T(1,128)}, f32[1,144]{1,0:T(1,128)}, f32[144,288]{1,0:T(8,128)}...) custom-call(bf16[128,1152]{1,0:T(8,128)(2,1)} %bitcast.8, ...), custom_call_target="tpu_custom_call" | custom-call | tf_op jit(solution)/shard_map/layer/pallas_call | solution.py:1380
  231.3 3.3 %hand_over.1 = (bf16[128,1152]{1,0:T(8,128)(2,1)}, bf16[128,1152]{1,0:T(8,128)(2,1)}, f32[1,144]{1,0:T(1,128)}, f32[1,144]{1,0:T(1,128)}, f32[144,288]{1,0:T(8,1...) custom-call(bf16[128,1152]{1,0:T(8,128)(2,1)} %get-tuple-element.33., ...), custom_call_target="tpu_custom_call" | custom-call | tf_op jit(solution)/shard_map/hand_over/pallas_call | solution.py:1392

commit v5 on v4

--- a/solution.py
+++ b/solution.py
@@ -699,6 +699,7 @@
     z_start(wo, lambda k: woz.at[k - 1], r_woz)
     spread_wo(0, wo)
     send_ff(0)
+    send_ff(1)
     gather_z(c8, r_c8)
 
     for k in range(4):
@@ -797,7 +798,6 @@
         for k in range(4):
             net.recv(kv_part(s, k, 1), r_kx + 4 * s + k)
 
-    send_ff(1)
     send_down()
 
     for t in range(qf.shape[1] // 128):
@@ -842,8 +842,14 @@
     gather_pass(c8, r_c8, 1)
     attend(0, 2)
     take_kv(1)
-    for g in range(groups):
-        attend(1, g)
+    attend(1, 0)
+    pass_ff(1)
+    attend(1, 1)
+    for cc in range(2):
+        part = wd8.at[pl.ds(off(2 * y + cc, drows), drows)]
+        net.recv(part, r_wd + cc)
+        net.send(part, part, r_wy + cc, dev(1 - y, c, z, x))
+    attend(1, 2)
 
     for hx, hy, cc in ((0, 0, 0), (0, 0, 1), (0, 1, 1), (1, 0, 0), (1, 1, 0), (1, 1, 1)):
         for zz in range(2):
@@ -857,11 +863,6 @@
             mp[s, :, qcols * part : qcols * (part + 1)] = got[s * tokens : (s + 1) * tokens]
     r_ml = net.slots(1)
     mp_sent = net.send(mp.at[1], ml, r_ml, partner)
-    pass_ff(1)
-    for cc in range(2):
-        part = wd8.at[pl.ds(off(2 * y + cc, drows), drows)]
-        net.recv(part, r_wd + cc)
-        net.send(part, part, r_wy + cc, dev(1 - y, c, z, x))
     gather_pass(c8, r_c8, 2)
     gather_pass(c8, r_c8, 3)
     net.recv(ml, r_ml)

time: 235 us -> 230 us (0.979)
  Pallas kernels: 233 us -> 229 us
    pallas_call x1, Pallas kernels: 230 us -> 225 us  [run_layer(): pl.pallas_call(layer_kernel, out_shape=out_shape, in_specs=[inside] * 3 +...]
where the time goes in v5:
time: 230 us
  Pallas kernels  229 us (100%)
    pallas_call x1, Pallas kernels, run_layer(): pl.pallas_call(layer_kernel, out_shape=out_shape, in_specs=[inside] * 3 +...  225 us

profile of v5, /device:TPU:0, one launch (start us, length us, event | category | flops | bytes accessed | tf_op | source)
XLA Modules:
  0.0 230.1 jit_solution(2709157942679072787)
XLA Ops:
  1.3 225.4 %layer.1 = (bf16[128,1152]{1,0:T(8,128)(2,1)}, bf16[128,1152]{1,0:T(8,128)(2,1)}, f32[1,144]{1,0:T(1,128)}, f32[1,144]{1,0:T(1,128)}, f32[144,288]{1,0:T(8,128)}...) custom-call(bf16[128,1152]{1,0:T(8,128)(2,1)} %bitcast.8, ...), custom_call_target="tpu_custom_call" | custom-call | tf_op jit(solution)/shard_map/layer/pallas_call | solution.py:1381
  226.7 3.3 %hand_over.1 = (bf16[128,1152]{1,0:T(8,128)(2,1)}, bf16[128,1152]{1,0:T(8,128)(2,1)}, f32[1,144]{1,0:T(1,128)}, f32[1,144]{1,0:T(1,128)}, f32[144,288]{1,0:T(8,1...) custom-call(bf16[128,1152]{1,0:T(8,128)(2,1)} %get-tuple-element.33., ...), custom_call_target="tpu_custom_call" | custom-call | tf_op jit(solution)/shard_map/hand_over/pallas_call | solution.py:1393

commit v6 on v5

--- a/solution.py
+++ b/solution.py
@@ -841,9 +841,9 @@
     attend(0, 1)
     gather_pass(c8, r_c8, 1)
     attend(0, 2)
+    pass_ff(1)
     take_kv(1)
     attend(1, 0)
-    pass_ff(1)
     attend(1, 1)
     for cc in range(2):
         part = wd8.at[pl.ds(off(2 * y + cc, drows), drows)]
@@ -964,22 +964,22 @@
             ggu.at[:, at], lgu.at[:, at], r_gz + zt, dev(1 - y, c, z, x),
             only=jnp.logical_not(home),
         )
+
+    total = dmid[...] + reduce_end(l2, r_dn)
+    normed_two, inv_two = normed(mid[...])
+    total = total * grow[1:2]
+    dmid[...] = cot[...].astype(F32) + inv_two * (
+        total - normed_two * jnp.mean(total * normed_two, -1, keepdims=True)
+    )
+    dmb[0] = dmid[...].astype(BF16)
+    r_dm = net.slots(1)
+    net.send(dmb.at[0], dmb.at[1], r_dm, partner)
     for finish in pt_sent:
         net.done(finish)
     lax.fori_loop(0, 4, feed_out, 0)
     r_out = net.slots(8)
     for h in range(4):
         reduce_start(pt, l1o, r_out, h)
-
-    total = dmid[...] + reduce_end(l2, r_dn)
-    normed_two, inv_two = normed(mid[...])
-    total = total * grow[1:2]
-    dmid[...] = cot[...].astype(F32) + inv_two * (
-        total - normed_two * jnp.mean(total * normed_two, -1, keepdims=True)
-    )
-    dmb[0] = dmid[...].astype(BF16)
-    r_dm = net.slots(1)
-    net.send(dmb.at[0], dmb.at[1], r_dm, partner)
 
     r_ld = net.slots(2)
     net.recv(lgd, r_gd)
@@ -1068,33 +1068,12 @@
     for g in range(groups):
         attend_back(0, g)
     send_dkv(0)
-    r_gf = net.slots(4)
-    for k in (3, 2, 1, 0):
-        at = pl.ds(off(zat(k), 2 * rows), 2 * rows)
-
-        @pl.when(home)
-        def _():
-            net.recv(lgu.at[:, at], r_gz + zat(k))
-            ggu[:, at] = (ggu[:, at].astype(F32) + lgu[:, at].astype(F32)).astype(BF16)
-
-        for hx in range(2):
-            src = ggu.at[:, pl.ds(off(2 * zat(k) + flip(x, hx), rows), rows)]
-            dst = lf.at[x, z_hi]
-            slot = r_gf + x * 2 + z_hi
-            if k + hx:
-                net.send(src, dst, slot, dev(y, c, zat(k), flip(x, hx)), only=home)
-            else:
-
-                @pl.when(home)
-                def _():
-                    net.keep(src, dst, slot)
-
     attend_back(1, 0)
-    pass_go()
     attend_back(1, 1)
     pass_dkv(0)
     attend_back(1, 2)
     send_dkv(1)
+    pass_go()
     for t in range(qf.shape[1] // 128):
         qf[:, 128 * t : 128 * (t + 1)] = turn(qf[:, 128 * t : 128 * (t + 1)], False)
     grad = dot_tn(n1[...], qf[:, 0:qw].astype(BF16)).astype(BF16)
@@ -1169,6 +1148,27 @@
 
     send_grads(in_p6, lqy, r_qy)
     pass_dkv(1)
+    r_gf = net.slots(4)
+    for k in (3, 2, 1, 0):
+        at = pl.ds(off(zat(k), 2 * rows), 2 * rows)
+
+        @pl.when(home)
+        def _():
+            net.recv(lgu.at[:, at], r_gz + zat(k))
+            ggu[:, at] = (ggu[:, at].astype(F32) + lgu[:, at].astype(F32)).astype(BF16)
+
+        for hx in range(2):
+            src = ggu.at[:, pl.ds(off(2 * zat(k) + flip(x, hx), rows), rows)]
+            dst = lf.at[x, z_hi]
+            slot = r_gf + x * 2 + z_hi
+            if k + hx:
+                net.send(src, dst, slot, dev(y, c, zat(k), flip(x, hx)), only=home)
+            else:
+
+                @pl.when(home)
+                def _():
+                    net.keep(src, dst, slot)
+
     for h in range(1, 4):
         reduce_pass(pt, l1o, s2o, l2o, r_out, h)
     mid[...] = mid[...] + reduce_own(pt, l1o, r_out)

time: 230 us -> 229 us (level)
  no operation moved by 1% of the time
where the time goes in v6:
time: 229 us
  Pallas kernels  227 us (99%)
    pallas_call x1, Pallas kernels, run_layer(): pl.pallas_call(layer_kernel, out_shape=out_shape, in_specs=[inside] * 3 +...  224 us

profile of v6, /device:TPU:0, one launch (start us, length us, event | category | flops | bytes accessed | tf_op | source)
XLA Modules:
  0.0 228.7 jit_solution(7102799979116342630)
XLA Ops:
  1.3 224.0 %layer.1 = (bf16[128,1152]{1,0:T(8,128)(2,1)}, bf16[128,1152]{1,0:T(8,128)(2,1)}, f32[1,144]{1,0:T(1,128)}, f32[1,144]{1,0:T(1,128)}, f32[144,288]{1,0:T(8,128)}...) custom-call(bf16[128,1152]{1,0:T(8,128)(2,1)} %bitcast.8, ...), custom_call_target="tpu_custom_call" | custom-call | tf_op jit(solution)/shard_map/layer/pallas_call | solution.py:1381
  225.3 3.3 %hand_over.1 = (bf16[128,1152]{1,0:T(8,128)(2,1)}, bf16[128,1152]{1,0:T(8,128)(2,1)}, f32[1,144]{1,0:T(1,128)}, f32[1,144]{1,0:T(1,128)}, f32[144,288]{1,0:T(8,1...) custom-call(bf16[128,1152]{1,0:T(8,128)(2,1)} %get-tuple-element.33., ...), custom_call_target="tpu_custom_call" | custom-call | tf_op jit(solution)/shard_map/hand_over/pallas_call | solution.py:1393

commit v7 on v6

--- a/solution.py
+++ b/solution.py
@@ -1085,14 +1085,14 @@
     mine = c == y
 
     def send_grads(source, land, slot):
-        for k in range(4):
+        for k in (1, 2, 3, 0):
             net.send(
                 source(zat(k), slice(0, 2)), land.at[zat(k)], slot + k, dev(1 - y, c, z, x),
                 only=jnp.logical_not(mine),
             )
 
     def add_y(source, land, slot, land_x, slot_x):
-        for k in range(4):
+        for k in (1, 2, 3, 0):
 
             @pl.when(mine)
             def _():

time: 229 us -> 229 us (level)
  no operation moved by 1% of the time
where the time goes in v7:
time: 229 us
  Pallas kernels  227 us (99%)
    pallas_call x1, Pallas kernels, run_layer(): pl.pallas_call(layer_kernel, out_shape=out_shape, in_specs=[inside] * 3 +...  224 us

profile of v7, /device:TPU:0, one launch (start us, length us, event | category | flops | bytes accessed | tf_op | source)
XLA Modules:
  0.0 228.7 jit_solution(7727655722753428857)
XLA Ops:
  1.3 224.0 %layer.1 = (bf16[128,1152]{1,0:T(8,128)(2,1)}, bf16[128,1152]{1,0:T(8,128)(2,1)}, f32[1,144]{1,0:T(1,128)}, f32[1,144]{1,0:T(1,128)}, f32[144,288]{1,0:T(8,128)}...) custom-call(bf16[128,1152]{1,0:T(8,128)(2,1)} %bitcast.8, ...), custom_call_target="tpu_custom_call" | custom-call | tf_op jit(solution)/shard_map/layer/pallas_call | solution.py:1381
  225.3 3.3 %hand_over.1 = (bf16[128,1152]{1,0:T(8,128)(2,1)}, bf16[128,1152]{1,0:T(8,128)(2,1)}, f32[1,144]{1,0:T(1,128)}, f32[1,144]{1,0:T(1,128)}, f32[144,288]{1,0:T(8,1...) custom-call(bf16[128,1152]{1,0:T(8,128)(2,1)} %get-tuple-element.33., ...), custom_call_target="tpu_custom_call" | custom-call | tf_op jit(solution)/shard_map/hand_over/pallas_call | solution.py:1393
